TPU v7x, 32 devices: a whole 2x2x4 slice. The times are simulated.
32 devices in a mesh: dp: 4 (over x, core), fsdp: 8 (over z, y).
Axes of the slice: x: 2, y: 2, z: 4, core: 2. Of those that a mesh axis runs over, the one named last changes fastest.
Arguments:
- tokens: bfloat16 [32768, 768], P(('dp', 'fsdp')), may hold values from -6 to 6
- lengths: int32 [64], P(('dp', 'fsdp')), may hold values from 16 to 512, as said below
- labels: int32 [64], P(('dp', 'fsdp')), may hold values from 0 to 2
- cotangent: bfloat16 [32768, 768], P(('dp', 'fsdp')), may hold values from -6 to 6
- qkv_weight: bfloat16 [768, 2304], P('fsdp'), may hold values from -0.21875 to 0.21875
- query_bias: bfloat16 [768], P('fsdp'), may hold values from -1.1953125 to 1.1953125
- value_bias: bfloat16 [768], P('fsdp'), may hold values from -1.1953125 to 1.1953125
- out_weight: bfloat16 [768, 768], P('fsdp'), may hold values from -1.75 to 1.75
- out_bias: bfloat16 [768], P('fsdp'), may hold values from -1.1953125 to 1.1953125
- first_gain: bfloat16 [768], P('fsdp'), may hold values from 0.5 to 1.5
- first_shift: bfloat16 [768], P('fsdp'), may hold values from -1.1953125 to 1.1953125
- inner_weight: bfloat16 [768, 3072], P('fsdp'), may hold values from -0.21875 to 0.21875
- inner_bias: bfloat16 [3072], P('fsdp'), may hold values from -1.1953125 to 1.1953125
- outer_weight: bfloat16 [3072, 768], P('fsdp'), may hold values from -0.15625 to 0.15625
- outer_bias: bfloat16 [768], P('fsdp'), may hold values from -1.1953125 to 1.1953125
- second_gain: bfloat16 [768], P('fsdp'), may hold values from 0.5 to 1.5
- second_shift: bfloat16 [768], P('fsdp'), may hold values from -1.1953125 to 1.1953125
- pool_weight: bfloat16 [768, 768], P('fsdp'), may hold values from -0.21875 to 0.21875
- pool_bias: bfloat16 [768], P('fsdp'), may hold values from -1.1953125 to 1.1953125
- class_weight: bfloat16 [768, 3], P('fsdp'), may hold values from -0.21875 to 0.21875
- class_bias: bfloat16 [3], replicated, may hold values from -2 to 2
Outputs:
- output: bfloat16 [32768, 768], P(('dp', 'fsdp'))
- exit_loss: float32 [64], P(('dp', 'fsdp'))
- tokens_grad: bfloat16 [32768, 768], P(('dp', 'fsdp'))
- qkv_weight_grad: float32 [768, 2304], P('fsdp')
- query_bias_grad: float32 [768], P('fsdp')
- value_bias_grad: float32 [768], P('fsdp')
- out_weight_grad: float32 [768, 768], P('fsdp')
- out_bias_grad: float32 [768], P('fsdp')
- first_gain_grad: float32 [768], P('fsdp')
- first_shift_grad: float32 [768], P('fsdp')
- inner_weight_grad: float32 [768, 3072], P('fsdp')
- inner_bias_grad: float32 [3072], P('fsdp')
- outer_weight_grad: float32 [3072, 768], P('fsdp')
- outer_bias_grad: float32 [768], P('fsdp')
- second_gain_grad: float32 [768], P('fsdp')
- second_shift_grad: float32 [768], P('fsdp')
- pool_weight_grad: float32 [768, 768], P('fsdp')
- pool_bias_grad: float32 [768], P('fsdp')
- class_weight_grad: float32 [768, 3], P('fsdp')
- class_bias_grad: float32 [3], replicated
Inputs may be any that keep to these rules, and one draw needn't show every extreme that they name: `lengths`: true tokens of each sequence; some sequence has exactly 512 and another exactly 16.
All inputs are finite; a program needn't handle non-finite values.
Results may differ from a plain program's by a relative error of at most 0.015.
Values may be sent and summed in bfloat16 or wider, within the bound.
A program may use at most 192 MiB of HBM per device.

v0:
```python
import jax
import jax.numpy as jnp
from jax import lax
from jax.sharding import PartitionSpec as P

HEADS = 12


EPS = 1e-12
NEG = -1000000000.0


def normalize(value, gain, shift):
    mean = jnp.mean(value, axis=-1, keepdims=True)
    centred = value - mean
    inverse = lax.rsqrt(jnp.mean(centred * centred, axis=-1, keepdims=True) + EPS)
    unit = centred * inverse
    return (unit * gain + shift, unit, inverse)


def norm_back(grad, unit, inverse, gain):
    scaled = grad * gain
    inner = (
        scaled
        - jnp.mean(scaled, axis=-1, keepdims=True)
        - unit * jnp.mean(scaled * unit, axis=-1, keepdims=True)
    )
    return (inner * inverse, jnp.sum(grad * unit, axis=0), jnp.sum(grad, axis=0))


def matmul(left, right):
    return jnp.dot(left, right, preferred_element_type=jnp.float32)


def transposed_left(left, right):
    return lax.dot_general(
        left, right, (((0,), (0,)), ((), ())), preferred_element_type=jnp.float32
    )


def transposed_right(left, right):
    return lax.dot_general(
        left, right, (((1,), (1,)), ((), ())), preferred_element_type=jnp.float32
    )


def column_sum(values):
    return jnp.sum(values.astype(jnp.float32), axis=0)


def attend(block):
    query, key, value, keep = block
    scale = query.shape[-1] ** (-0.5)
    scores = jnp.einsum("qhd,khd->hqk", query, key, preferred_element_type=jnp.float32) * scale
    scores = jnp.where(keep[None, None, :], scores, NEG)
    top = jnp.max(scores, axis=-1, keepdims=True)
    total = jnp.sum(jnp.exp(scores - top), axis=-1, keepdims=True)
    logsum = top + jnp.log(total)
    probs = jnp.exp(scores - logsum).astype(jnp.bfloat16)
    context = jnp.einsum("hqk,khd->qhd", probs, value, preferred_element_type=jnp.float32)
    return (context.astype(jnp.bfloat16), logsum[:, :, 0])


def attend_back(block):
    query, key, value, keep, logsum, grad_context = block
    scale = query.shape[-1] ** (-0.5)
    scores = jnp.einsum("qhd,khd->hqk", query, key, preferred_element_type=jnp.float32) * scale
    scores = jnp.where(keep[None, None, :], scores, NEG)
    probs = jnp.exp(scores - logsum[:, :, None])
    grad_value = jnp.einsum(
        "hqk,qhd->khd", probs.astype(jnp.bfloat16), grad_context, preferred_element_type=jnp.float32
    )
    grad_probs = jnp.einsum("qhd,khd->hqk", grad_context, value, preferred_element_type=jnp.float32)
    delta = jnp.sum(grad_probs * probs, axis=-1, keepdims=True)
    grad_scores = (probs * (grad_probs - delta)).astype(jnp.bfloat16)
    grad_query = (
        jnp.einsum("hqk,khd->qhd", grad_scores, key, preferred_element_type=jnp.float32) * scale
    )
    grad_key = (
        jnp.einsum("hqk,qhd->khd", grad_scores, query, preferred_element_type=jnp.float32) * scale
    )
    return (
        grad_query.astype(jnp.bfloat16),
        grad_key.astype(jnp.bfloat16),
        grad_value.astype(jnp.bfloat16),
    )


def per_device(
    tokens,
    lengths,
    labels,
    cotangent,
    qkv_weight,
    query_bias,
    value_bias,
    out_weight,
    out_bias,
    first_gain,
    first_shift,
    inner_weight,
    inner_bias,
    outer_weight,
    outer_bias,
    second_gain,
    second_shift,
    pool_weight,
    pool_bias,
    class_weight,
    class_bias,
):
    full = (
        lax.all_gather(qkv_weight, "fsdp", axis=0, tiled=True),
        lax.all_gather(query_bias, "fsdp", axis=0, tiled=True),
        lax.all_gather(value_bias, "fsdp", axis=0, tiled=True),
        lax.all_gather(out_weight, "fsdp", axis=0, tiled=True),
        lax.all_gather(out_bias, "fsdp", axis=0, tiled=True),
        lax.all_gather(first_gain, "fsdp", axis=0, tiled=True),
        lax.all_gather(first_shift, "fsdp", axis=0, tiled=True),
        lax.all_gather(inner_weight, "fsdp", axis=0, tiled=True),
        lax.all_gather(inner_bias, "fsdp", axis=0, tiled=True),
        lax.all_gather(outer_weight, "fsdp", axis=0, tiled=True),
        lax.all_gather(outer_bias, "fsdp", axis=0, tiled=True),
        lax.all_gather(second_gain, "fsdp", axis=0, tiled=True),
        lax.all_gather(second_shift, "fsdp", axis=0, tiled=True),
        lax.all_gather(pool_weight, "fsdp", axis=0, tiled=True),
        lax.all_gather(pool_bias, "fsdp", axis=0, tiled=True),
        lax.all_gather(class_weight, "fsdp", axis=0, tiled=True),
    )
    (
        w_qkv,
        b_query,
        b_value,
        w_out,
        b_out,
        g_first,
        s_first,
        w_inner,
        b_inner,
        w_outer,
        b_outer,
        g_second,
        s_second,
        w_pool,
        b_pool,
        w_class,
    ) = full
    b_query = b_query.astype(jnp.float32)
    b_value = b_value.astype(jnp.float32)
    b_out = b_out.astype(jnp.float32)
    g_first = g_first.astype(jnp.float32)
    s_first = s_first.astype(jnp.float32)
    b_inner = b_inner.astype(jnp.float32)
    b_outer = b_outer.astype(jnp.float32)
    g_second = g_second.astype(jnp.float32)
    s_second = s_second.astype(jnp.float32)
    b_pool = b_pool.astype(jnp.float32)
    b_class = class_bias.astype(jnp.float32)
    seqs = lengths.shape[0]
    rows, width = tokens.shape
    span = rows // seqs
    size = width // HEADS
    classes = class_bias.shape[0]
    position = lax.broadcasted_iota(jnp.int32, (seqs, span), 1)
    keep = position < lengths[:, None]
    valid = keep.reshape(rows, 1).astype(jnp.float32)
    bias_all = jnp.concatenate([b_query, jnp.zeros_like(b_query), b_value])
    qkv = (matmul(tokens, w_qkv) + bias_all).astype(jnp.bfloat16)
    query = qkv[:, :width].reshape(seqs, span, HEADS, size)
    key = qkv[:, width : 2 * width].reshape(seqs, span, HEADS, size)
    value = qkv[:, 2 * width :].reshape(seqs, span, HEADS, size)
    context, logsum = lax.map(attend, (query, key, value, keep))
    context = context.reshape(rows, width)
    attended = matmul(context, w_out) + b_out
    hidden, unit_first, inverse_first = normalize(
        tokens.astype(jnp.float32) + attended, g_first, s_first
    )
    hidden_low = hidden.astype(jnp.bfloat16)
    inner = matmul(hidden_low, w_inner) + b_inner
    act = jax.nn.gelu(inner, approximate=False).astype(jnp.bfloat16)
    ffn = matmul(act, w_outer) + b_outer
    layer, unit_second, inverse_second = normalize(hidden + ffn, g_second, s_second)
    output = (layer * valid).astype(jnp.bfloat16)
    first = layer.reshape(seqs, span, width)[:, 0].astype(jnp.bfloat16)
    pooled = jnp.tanh(matmul(first, w_pool) + b_pool)
    pooled_low = pooled.astype(jnp.bfloat16)
    logits = matmul(pooled_low, w_class) + b_class
    peak = jnp.max(logits, axis=-1, keepdims=True)
    logsum_class = peak + jnp.log(jnp.sum(jnp.exp(logits - peak), axis=-1, keepdims=True))
    onehot = (labels[:, None] == lax.broadcasted_iota(jnp.int32, (seqs, classes), 1)).astype(
        jnp.float32
    )
    exit_loss = logsum_class[:, 0] - jnp.sum(onehot * logits, axis=-1)
    again = (
        lax.all_gather(qkv_weight, "fsdp", axis=0, tiled=True),
        lax.all_gather(query_bias, "fsdp", axis=0, tiled=True),
        lax.all_gather(value_bias, "fsdp", axis=0, tiled=True),
        lax.all_gather(out_weight, "fsdp", axis=0, tiled=True),
        lax.all_gather(out_bias, "fsdp", axis=0, tiled=True),
        lax.all_gather(first_gain, "fsdp", axis=0, tiled=True),
        lax.all_gather(first_shift, "fsdp", axis=0, tiled=True),
        lax.all_gather(inner_weight, "fsdp", axis=0, tiled=True),
        lax.all_gather(inner_bias, "fsdp", axis=0, tiled=True),
        lax.all_gather(outer_weight, "fsdp", axis=0, tiled=True),
        lax.all_gather(outer_bias, "fsdp", axis=0, tiled=True),
        lax.all_gather(second_gain, "fsdp", axis=0, tiled=True),
        lax.all_gather(second_shift, "fsdp", axis=0, tiled=True),
        lax.all_gather(pool_weight, "fsdp", axis=0, tiled=True),
        lax.all_gather(pool_bias, "fsdp", axis=0, tiled=True),
        lax.all_gather(class_weight, "fsdp", axis=0, tiled=True),
    )
    w_qkv = again[0]
    w_out = again[3]
    g_first = again[5].astype(jnp.float32)
    w_inner = again[7]
    w_outer = again[9]
    g_second = again[11].astype(jnp.float32)
    w_pool = again[13]
    w_class = again[15]
    grad_logits = (jnp.exp(logits - logsum_class) - onehot).astype(jnp.bfloat16)
    grad_class_weight = transposed_left(pooled_low, grad_logits)
    grad_class_local = column_sum(grad_logits)
    grad_pooled = transposed_right(grad_logits, w_class)
    grad_pre = (grad_pooled * (1.0 - pooled * pooled)).astype(jnp.bfloat16)
    grad_pool_weight = transposed_left(first, grad_pre)
    grad_pool_bias = column_sum(grad_pre)
    grad_first = transposed_right(grad_pre, w_pool)
    grad_layer = (cotangent.astype(jnp.float32) * valid).reshape(seqs, span, width)
    grad_layer = jnp.concatenate(
        [grad_layer[:, :1] + grad_first[:, None, :], grad_layer[:, 1:]], axis=1
    )
    grad_layer = grad_layer.reshape(rows, width)
    grad_resid_second, grad_second_gain, grad_second_shift = norm_back(
        grad_layer, unit_second, inverse_second, g_second
    )
    grad_ffn = grad_resid_second.astype(jnp.bfloat16)
    grad_outer_weight = transposed_left(act, grad_ffn)
    grad_outer_bias = column_sum(grad_ffn)
    grad_act = transposed_right(grad_ffn, w_outer)
    gelu_value, gelu_pull = jax.vjp(lambda v: jax.nn.gelu(v, approximate=False), inner)
    grad_inner = gelu_pull(grad_act)[0].astype(jnp.bfloat16)
    grad_inner_weight = transposed_left(hidden_low, grad_inner)
    grad_inner_bias = column_sum(grad_inner)
    grad_hidden = grad_resid_second + transposed_right(grad_inner, w_inner)
    grad_resid_first, grad_first_gain, grad_first_shift = norm_back(
        grad_hidden, unit_first, inverse_first, g_first
    )
    grad_attended = grad_resid_first.astype(jnp.bfloat16)
    grad_out_weight = transposed_left(context, grad_attended)
    grad_out_bias = column_sum(grad_attended)
    grad_context = (
        transposed_right(grad_attended, w_out).astype(jnp.bfloat16).reshape(seqs, span, HEADS, size)
    )
    grad_query, grad_key, grad_value = lax.map(
        attend_back, (query, key, value, keep, logsum, grad_context)
    )
    grad_query = grad_query.reshape(rows, width)
    grad_key = grad_key.reshape(rows, width)
    grad_value = grad_value.reshape(rows, width)
    grad_qkv = jnp.concatenate([grad_query, grad_key, grad_value], axis=1)
    grad_qkv_weight = transposed_left(tokens, grad_qkv)
    grad_query_bias = column_sum(grad_query)
    grad_value_bias = column_sum(grad_value)
    tokens_grad = (grad_resid_first + transposed_right(grad_qkv, w_qkv)).astype(jnp.bfloat16)
    owned = (
        lax.psum_scatter(grad_qkv_weight, "fsdp", scatter_dimension=0, tiled=True),
        lax.psum_scatter(grad_query_bias, "fsdp", scatter_dimension=0, tiled=True),
        lax.psum_scatter(grad_value_bias, "fsdp", scatter_dimension=0, tiled=True),
        lax.psum_scatter(grad_out_weight, "fsdp", scatter_dimension=0, tiled=True),
        lax.psum_scatter(grad_out_bias, "fsdp", scatter_dimension=0, tiled=True),
        lax.psum_scatter(grad_first_gain, "fsdp", scatter_dimension=0, tiled=True),
        lax.psum_scatter(grad_first_shift, "fsdp", scatter_dimension=0, tiled=True),
        lax.psum_scatter(grad_inner_weight, "fsdp", scatter_dimension=0, tiled=True),
        lax.psum_scatter(grad_inner_bias, "fsdp", scatter_dimension=0, tiled=True),
        lax.psum_scatter(grad_outer_weight, "fsdp", scatter_dimension=0, tiled=True),
        lax.psum_scatter(grad_outer_bias, "fsdp", scatter_dimension=0, tiled=True),
        lax.psum_scatter(grad_second_gain, "fsdp", scatter_dimension=0, tiled=True),
        lax.psum_scatter(grad_second_shift, "fsdp", scatter_dimension=0, tiled=True),
        lax.psum_scatter(grad_pool_weight, "fsdp", scatter_dimension=0, tiled=True),
        lax.psum_scatter(grad_pool_bias, "fsdp", scatter_dimension=0, tiled=True),
        lax.psum_scatter(grad_class_weight, "fsdp", scatter_dimension=0, tiled=True),
    )
    summed = lax.psum(
        (
            owned[0],
            owned[1],
            owned[2],
            owned[3],
            owned[4],
            owned[5],
            owned[6],
            owned[7],
            owned[8],
            owned[9],
            owned[10],
            owned[11],
            owned[12],
            owned[13],
            owned[14],
            owned[15],
        ),
        "dp",
    )
    class_bias_grad = lax.psum(grad_class_local, ("dp", "fsdp"))
    return (
        output,
        exit_loss,
        tokens_grad,
        summed[0],
        summed[1],
        summed[2],
        summed[3],
        summed[4],
        summed[5],
        summed[6],
        summed[7],
        summed[8],
        summed[9],
        summed[10],
        summed[11],
        summed[12],
        summed[13],
        summed[14],
        summed[15],
        class_bias_grad,
    )


def solution(mesh):
    in_specs = (
        P(("dp", "fsdp"), None),
        P(("dp", "fsdp")),
        P(("dp", "fsdp")),
        P(("dp", "fsdp"), None),
        P("fsdp", None),
        P("fsdp"),
        P("fsdp"),
        P("fsdp", None),
        P("fsdp"),
        P("fsdp"),
        P("fsdp"),
        P("fsdp", None),
        P("fsdp"),
        P("fsdp", None),
        P("fsdp"),
        P("fsdp"),
        P("fsdp"),
        P("fsdp", None),
        P("fsdp"),
        P("fsdp", None),
        P(),
    )
    out_specs = (
        P(("dp", "fsdp"), None),
        P(("dp", "fsdp")),
        P(("dp", "fsdp"), None),
        P("fsdp", None),
        P("fsdp"),
        P("fsdp"),
        P("fsdp", None),
        P("fsdp"),
        P("fsdp"),
        P("fsdp"),
        P("fsdp", None),
        P("fsdp"),
        P("fsdp", None),
        P("fsdp"),
        P("fsdp"),
        P("fsdp"),
        P("fsdp", None),
        P("fsdp"),
        P("fsdp", None),
        P(),
    )
    return jax.shard_map(
        per_device, mesh=mesh, in_specs=in_specs, out_specs=out_specs, check_vma=False
    )
```

profile of v0, /device:TPU:0, one launch (start us, length us, event | category | flops | bytes accessed | tf_op | source)
XLA Modules:
  0.0 1223.3 jit_solution(9411809324162300262)
XLA Ops:
  22.0 39.8 %all-reduce.22 = (bf16[768]{0:T(1024)(128)(2,1)S(1)}, bf16[768]{0:T(1024)(128)(2,1)S(1)}, bf16[768]{0:T(1024)(128)(2,1)S(1)}, bf16[768]{0:T(1024)(128)(2,1)S(1)}...) all-reduce(bf16[768]{0:T(1024)(128)(2,1)S(1)} %dynamic-update-slice, ...), channel_id=1, replica_groups=mesh['dp'=4,'fsdp'=8] {'fsdp'}, use_global_device_ids=true, to_apply=%add.1 | all-reduce | flops 6912 | bytes 27648
  65.5 16.6 %all-gather.1 = bf16[8,96,3]{1,2,0:T(4,128)(2,1)S(1)} all-gather(bf16[1,96,3]{1,2,0:T(4,128)(2,1)} %bitcast.207), channel_id=1, replica_groups=mesh['dp'=4,'fsdp'=8] {'fsdp'}, dimensions={0}, use_global_device_ids=true | all-gather | bytes 5184 | tf_op jit(solution)/shard_map/all_gather | solution.py:128
  82.8 26.2 %all-gather = bf16[8,1,384]{2,1,0:T(2,128)(2,1)S(1)} all-gather(bf16[1,1,384]{2,1,0:T(2,128)(2,1)S(1)} %reshape.238), channel_id=1, replica_groups=mesh['dp'=4,'fsdp'=8] {'fsdp'}, dimensions={0}, use_global_device_ids=true | all-gather | bytes 6912 | tf_op jit(solution)/shard_map/all_gather | solution.py:121
  142.2 19.2 %while.26 = (s32[]{:T(128)}, bf16[2,512,12,64]{1,3,2,0:T(8,128)(2,1)}, f32[2,12,512]{2,1,0:T(8,128)S(1)}, bf16[2,512,12,64]{1,3,2,0:T(8,128)(2,1)}, pred[2,512]{...) while((s32[]{:T(128)}, ...), condition=%wide.region_3.4_spmd, body=%wide.region_0.3_spmd.sunk | while | flops 840296448 | bytes 47428224 | solution.py:172
  171.7 30.0 %all-gather.12.cloned.1.call-done = bf16[768,3072]{1,0:T(8,128)(2,1)} async-done(((bf16[96,3072]{1,0:T(8,128)(2,1)}), bf16[768,3072]{1,0:T(8,128)(2,1)}) %all-gather.12.cloned.1.call-update) | async-done | bytes 4718608 | tf_op jit(solution)/shard_map/all_gather | solution.py:120
  201.6 35.8 %multiply_convert_fusion.3 = (bf16[1024,3072]{1,0:T(8,128)(2,1)}, f32[1024,3072]{1,0:T(8,128)}, f32[1024,3072]{1,0:T(8,128)}) fusion(f32[3072]{0:T(1024)S(1)} %bitcast.205, bf16[768,3072]{1,0:T(8,128)(2,1)} %all-gather.12.cloned.1.call-done, f32[1024,768]{1,0:T(8,128)S(1)} %get-tuple-element.336, f32[768]{0:T(1024)S(1)} %convert_element_type.157, ...), kind=kOutput, calls=%fused_computation.67 | convolution fusion | flops 5043388416 | bytes 39348224 | tf_op jit(solution)/shard_map/dot_general | solution.py:32
  237.4 44.3 %all-gather.14.cloned.1.call-done = bf16[3072,768]{1,0:T(8,128)(2,1)} async-done(((bf16[384,768]{1,0:T(8,128)(2,1)}), bf16[3072,768]{1,0:T(8,128)(2,1)}) %all-gather.14.cloned.1.call-update) | async-done | bytes 4718608 | tf_op jit(solution)/shard_map/all_gather | solution.py:122
  281.7 9.3 fusion.88
  297.6 25.4 %all-gather.16.cloned.1.call-done = bf16[768,768]{1,0:T(8,128)(2,1)} async-done(((bf16[96,768]{1,0:T(8,128)(2,1)}), bf16[768,768]{1,0:T(8,128)(2,1)}) %all-gather.16.cloned.1.call-update) | async-done | bytes 1179664 | tf_op jit(solution)/shard_map/all_gather | solution.py:126
  336.3 19.5 %convert_reduce_fusion = (f32[3072]{0:T(1024)}, bf16[1024,3072]{1,0:T(8,128)(2,1)}) fusion(f32[1024,3072]{1,0:T(8,128)} %get-tuple-element.318, bf16[3072,768]{1,0:T(8,128)(2,1)} %all-gather.14.cloned.1.call-done, f32[1024,768]{1,0:T(8,128)} %get-tuple-element.310, f32[1024,3072]{1,0:T(8,128)} %get-tuple-element.337, f32[3072]{0:T(1024)S(1)} %bitcast.206), kind=kOutput, calls=%fused_computation.65 | convolution fusion | flops 4886098944 | bytes 39346176 | tf_op jit(solution)/shard_map/dot_general | solution.py:42
  355.8 10.6 multiply_reduce_fusion.1
  379.0 48.1 %while.27 = (s32[]{:T(128)}, bf16[2,512,12,64]{1,3,2,0:T(8,128)(2,1)}, bf16[2,512,12,64]{1,3,2,0:T(8,128)(2,1)}, bf16[2,512,12,64]{1,3,2,0:T(8,128)(2,1)}, bf16[...) while((s32[]{:T(128)}, ...), condition=%wide.region_17.18_spmd, body=%wide.region_15.17_spmd.sunk | while | flops 2062411776 | bytes 152764272 | solution.py:254
  443.1 8.0 copy.107
  460.1 10.5 fusion.76
  472.5 10.7 fusion.79
  485.0 94.1 %reduce-scatter.19.cloned.1.call-done = f32[96,2304]{1,0:T(8,128)} async-done(((f32[768,2304]{1,0:T(8,128)}), f32[96,2304]{1,0:T(8,128)}) %reduce-scatter.19.cloned.1.call-update) | async-done | bytes 884752
  581.7 69.4 %reduce-scatter.11.cloned.1.call-done = f32[96,768]{1,0:T(8,128)} async-done(((f32[768,768]{1,0:T(8,128)}), f32[96,768]{1,0:T(8,128)}) %reduce-scatter.11.cloned.1.call-update) | async-done | bytes 294928 | tf_op jit(solution)/shard_map/reduce_scatter | solution.py:269
  651.1 71.9 %reduce-scatter.17.cloned.1.call-done = f32[96,768]{1,0:T(8,128)} async-done(((f32[768,768]{1,0:T(8,128)}), f32[96,768]{1,0:T(8,128)}) %reduce-scatter.17.cloned.1.call-update) | async-done | bytes 294928 | tf_op jit(solution)/shard_map/reduce_scatter | solution.py:279
  723.0 166.6 %reduce-scatter.15.cloned.1.call-done = f32[384,768]{1,0:T(8,128)} async-done(((f32[3072,768]{1,0:T(8,128)}), f32[384,768]{1,0:T(8,128)}) %reduce-scatter.15.cloned.1.call-update) | async-done | bytes 1179664 | tf_op jit(solution)/shard_map/reduce_scatter | solution.py:275
  889.6 166.5 %reduce-scatter.13.cloned.1.call-done = f32[96,3072]{1,0:T(8,128)} async-done(((f32[768,3072]{1,0:T(8,128)}), f32[96,3072]{1,0:T(8,128)}) %reduce-scatter.13.cloned.1.call-update) | async-done | bytes 1179664 | tf_op jit(solution)/shard_map/reduce_scatter | solution.py:273
  1057.4 39.5 %psum.135 = f32[3]{0:T(128)} all-reduce(f32[3]{0:T(128)S(1)} %copy-done.64), channel_id=1, replica_groups=mesh['dp'=4,'fsdp'=8] {'dp','fsdp'}, use_global_device_ids=true, to_apply=%region_62.63 | all-reduce | flops 3 | bytes 24 | tf_op jit(solution)/shard_map/psum | solution.py:304
  1097.7 37.6 %all-reduce.19 = (f32[768]{0:T(1024)S(1)}, f32[768]{0:T(1024)S(1)}, f32[768]{0:T(1024)S(1)}, f32[768]{0:T(1024)S(1)}, f32[768]{0:T(1024)S(1)}, /*index=5*/f32[30...) all-reduce(f32[768]{0:T(1024)S(1)} %reduce_sum.230, ...), channel_id=3, replica_groups=mesh['dp'=4,'fsdp'=8] {'fsdp'}, use_global_device_ids=true, to_apply=%region_21.22.clone | all-reduce | flops 9984 | bytes 79872
  1136.1 9.4 add_convert_fusion.2
  1154.1 54.7 %all-reduce.25.cloned.1.call-done = (f32[96,2304]{0,1:T(8,128)}, f32[96,768]{1,0:T(8,128)}, f32[96,3072]{1,0:T(8,128)}, f32[384,768]{1,0:T(8,128)}, f32[96,768]{1,0:T(8,128)}) async-done(((f32[96,2304]{0,1:T(8,128)}, f32[96,768]{1,0:T(8,128)}, f32[96,3072]{1,0:T(8,128)}, f32[384,768]{1,0:T(8,128)}, f32[96,768]{1,0:T(8,128)}), (f32[96,2304]{0,1:T(8,128)}, f32[96,768]{1,0:T(8,128)}, f32[96,3072]{1,0:T(8,128)}, ...) | async-done | bytes 3833872 | tf_op jit(solution)/shard_map/psum | solution.py:283
  (329 shorter events, 208.8 us)
Async XLA Ops:
  7.2 101.9 %all-gather.8.cloned.1.call-start = ((), (), s32[]{:S(2)}) async-start(), calls=%async_computation.6 | async-start | bytes 3981312 | tf_op jit(solution)/shard_map/all_gather | solution.py:113
  7.9 159.3 %all-gather.10.cloned.1.call-start = ((), (), s32[]{:S(2)}) async-start(), calls=%async_computation.7 | async-start | bytes 1327104 | tf_op jit(solution)/shard_map/all_gather | solution.py:116
  8.7 192.9 %all-gather.12.cloned.1.call-start = ((), (), s32[]{:S(2)}) async-start(), calls=%async_computation.8 | async-start | bytes 5308416 | tf_op jit(solution)/shard_map/all_gather | solution.py:120
  9.4 272.3 %all-gather.14.cloned.1.call-start = ((), (), s32[]{:S(2)}) async-start(), calls=%async_computation.9 | async-start | bytes 5308416 | tf_op jit(solution)/shard_map/all_gather | solution.py:122
  10.0 313.0 %all-gather.16.cloned.1.call-start = ((), (), s32[]{:S(2)}) async-start(), calls=%async_computation.10 | async-start | bytes 1327104 | tf_op jit(solution)/shard_map/all_gather | solution.py:126
  10.6 568.6 %reduce-scatter.19.cloned.1.call-start = ((), (), s32[]{:S(2)}) async-start(), calls=%async_computation.15 | async-start | bytes 7962624
  61.8 304.6 %copy-start.37 = (f32[768]{0:T(1024)}, f32[768]{0:T(1024)S(1)}, u32[]{:S(2)}) copy-start(f32[768]{0:T(1024)S(1)} %convert_element_type.156) | copy-start | bytes 9220
  62.4 219.3 %copy-start.39 = (f32[768]{0:T(1024)}, f32[768]{0:T(1024)S(1)}, u32[]{:S(2)}) copy-start(f32[768]{0:T(1024)S(1)} %convert_element_type.157) | copy-start | bytes 9220
  171.1 66.3 %copy-start.4 = (f32[1024,768]{1,0:T(8,128)}, f32[1024,768]{1,0:T(8,128)S(1)}, u32[]{:S(2)}) copy-start(f32[1024,768]{1,0:T(8,128)S(1)} %get-tuple-element.336) | copy-start | bytes 9437188
  171.1 195.3 %copy-start.29 = (f32[1024]{0:T(1024)}, f32[1024]{0:T(1024)S(1)}, u32[]{:S(2)}) copy-start(f32[1024]{0:T(1024)S(1)} %broadcast_multiply_fusion.4) | copy-start | bytes 12292
  171.6 194.8 %copy-start.32 = (f32[1024]{0:T(1024)}, f32[1024]{0:T(1024)S(1)}, u32[]{:S(2)}) copy-start(f32[1024]{0:T(1024)S(1)} %add_rsqrt_fusion.1) | copy-start | bytes 12292
  201.6 80.1 %copy-start.60 = (f32[768]{0:T(1024)S(1)}, f32[768]{0:T(1024)}, u32[]{:S(2)}) copy-start(f32[768]{0:T(1024)} %convert_element_type.161) | copy-start | bytes 9220
  451.2 199.9 %reduce-scatter.11.cloned.1.call-start = ((), (), s32[]{:S(2)}) async-start(), calls=%async_computation.11 | async-start | bytes 2654208 | tf_op jit(solution)/shard_map/reduce_scatter | solution.py:269
  457.3 265.7 %reduce-scatter.17.cloned.1.call-start = ((), (), s32[]{:S(2)}) async-start(), calls=%async_computation.14 | async-start | bytes 2654208 | tf_op jit(solution)/shard_map/reduce_scatter | solution.py:279
  459.3 430.3 %reduce-scatter.15.cloned.1.call-start = ((), (), s32[]{:S(2)}) async-start(), calls=%async_computation.13 | async-start | bytes 10616832 | tf_op jit(solution)/shard_map/reduce_scatter | solution.py:275
  470.6 585.4 %reduce-scatter.13.cloned.1.call-start = ((), (), s32[]{:S(2)}) async-start(), calls=%async_computation.12 | async-start | bytes 10616832 | tf_op jit(solution)/shard_map/reduce_scatter | solution.py:273
  483.2 662.3 %reduce-scatter.21.cloned.1.call-start = ((), (), s32[]{:S(2)}) async-start(), calls=%async_computation.16 | async-start | bytes 442368
  484.9 572.5 %copy-start.64 = (f32[3]{0:T(128)S(1)}, f32[3]{0:T(128)}, u32[]{:S(2)}) copy-start(f32[3]{0:T(128)} %get-tuple-element.307) | copy-start | bytes 40
  485.0 612.0 %copy-start.13 = (bf16[2,512,12,64]{1,3,2,0:T(8,128)(2,1)S(1)}, bf16[2,512,12,64]{1,3,2,0:T(8,128)(2,1)}, u32[]{:S(2)}) copy-start(bf16[2,512,12,64]{1,3,2,0:T(8,128)(2,1)} %get-tuple-element.116) | copy-start | bytes 4718596
  485.0 723.8 %all-reduce.25.cloned.1.call-start = ((), (), s32[]{:S(2)}) async-start(), calls=%async_computation.17 | async-start | bytes 8257536 | tf_op jit(solution)/shard_map/psum | solution.py:283
  581.7 515.6 %copy-start.17 = (bf16[2,512,12,64]{1,3,2,0:T(8,128)(2,1)S(1)}, bf16[2,512,12,64]{1,3,2,0:T(8,128)(2,1)}, u32[]{:S(2)}) copy-start(bf16[2,512,12,64]{1,3,2,0:T(8,128)(2,1)} %get-tuple-element.114) | copy-start | bytes 4718596
  1056.0 41.6 %copy-start.53 = (f32[3072]{0:T(1024)S(1)}, f32[3072]{0:T(1024)}, u32[]{:S(2)}) copy-start(f32[3072]{0:T(1024)} %get-tuple-element.343) | copy-start | bytes 36868
  1056.1 41.6 %copy-start.57 = (f32[768]{0:T(1024)S(1)}, f32[768]{0:T(1024)}, u32[]{:S(2)}) copy-start(f32[768]{0:T(1024)} %get-tuple-element.347) | copy-start | bytes 9220
  1056.1 41.6 %copy-start.58 = (f32[768]{0:T(1024)S(1)}, f32[768]{0:T(1024)}, u32[]{:S(2)}) copy-start(f32[768]{0:T(1024)} %get-tuple-element.230) | copy-start | bytes 9220
  (65 other events, 585.3 us)
Sparse Core Ops, SparseCore 0:
  10.2 68.5 all-gather.7
  81.0 39.6 all-gather.9
  122.9 78.6 all-gather.11
  203.7 78.0 all-gather.13
  283.7 39.1 all-gather.15
  451.3 127.7 reduce-scatter.18
  583.0 68.0 reduce-scatter.10
  655.0 67.9 reduce-scatter.16
  727.0 162.4 reduce-scatter.14
  893.4 162.5 reduce-scatter.12
  1060.2 60.5 reduce-scatter.20
  1124.2 84.5 all-reduce.24
where the time goes:
time: 1230 us; the launch traced here: 1220 us
  waiting for transfers between devices  726 us (59%)
  matrix products  180 us (15%)
  blocking collectives  167 us (14%)
  local copies, waits for them, and re-layouts  90.8 us (7%)
  other arithmetic  40.9 us (3%)
  between operations  17.4 us (1%)
    reduce_scatter x1, waiting for transfers between devices, per_device(): lax.psum_scatter(grad_outer_weight, 'fsdp', scatter_dimension=0, tiled=True)  167 us
    reduce_scatter x1, waiting for transfers between devices, per_device(): lax.psum_scatter(grad_inner_weight, 'fsdp', scatter_dimension=0, tiled=True)  166 us
    unnamed x14, waiting for transfers between devices  97.4 us
    unnamed x2, blocking collectives  77.4 us
    reduce_scatter x1, waiting for transfers between devices, per_device(): lax.psum_scatter(grad_pool_weight, 'fsdp', scatter_dimension=0, tiled=True)  71.9 us
    reduce_scatter x1, waiting for transfers between devices, per_device(): lax.psum_scatter(grad_out_weight, 'fsdp', scatter_dimension=0, tiled=True)  69.4 us
    dot_general x6, matrix products, matmul(): return jnp.dot(left, right, preferred_element_type=jnp.float32)  57.1 us
    psum x1, waiting for transfers between devices, per_device(): lax.psum((owned[0], owned[1], owned[2], owned[3], owned[4], owned[5], own...  54.7 us
  transfers between devices with their start and end apart: 12, of which 9 were waited for; matrix products, arithmetic and copies ran while one was open for 14% of the time, Pallas kernels for 0%

commit v1 on v0

--- a/solution.py
+++ b/solution.py
@@ -1,13 +1,485 @@
+import functools
+import math
+
 import jax
 import jax.numpy as jnp
 from jax import lax
+from jax.experimental import pallas as pl
+from jax.experimental.pallas import tpu as pltpu
 from jax.sharding import PartitionSpec as P
 
 HEADS = 12
-
-
 EPS = 1e-12
 NEG = -1000000000.0
+F32 = jnp.float32
+BF16 = jnp.bfloat16
+MESH = pl.DeviceIdType.MESH
+LOG2E = math.log2(math.e)
+
+
+def nn(left, right):
+    return jnp.dot(left, right, preferred_element_type=F32)
+
+
+def nt(left, right):
+    return lax.dot_general(left, right, (((1,), (1,)), ((), ())), preferred_element_type=F32)
+
+
+def tn(left, right):
+    return lax.dot_general(left, right, (((0,), (0,)), ((), ())), preferred_element_type=F32)
+
+
+def rowmean(value):
+    return jnp.sum(value, axis=-1, keepdims=True) * (1.0 / value.shape[-1])
+
+
+def here():
+    d, f = lax.axis_index("dp"), lax.axis_index("fsdp")
+    return d // 2, d % 2, f // 2, f % 2
+
+
+def at(x, c, z, y):
+    return (x * 2 + c, z * 2 + y)
+
+
+def attend_forward(qkv, ctx, lse, lengths, i, span, width, size):
+    pairs = width // (2 * size)
+    wide = 2 * size
+    s, hp = i // pairs, i % pairs
+    rows = pl.ds(pl.multiple_of(s * span, span), span)
+
+    def part(p):
+        return qkv[rows, pl.ds(pl.multiple_of(p * width + hp * wide, wide), wide)]
+
+    q, k, v = part(0), part(1), part(2)
+    lane = lax.broadcasted_iota(jnp.int32, (span, wide), 1)
+    slot = lax.broadcasted_iota(jnp.int32, (span, wide), 0)
+    fill = jnp.where(slot < lengths[s], 0.0, NEG).astype(BF16)
+    vt = v.T
+    vrow = lax.broadcasted_iota(jnp.int32, (wide, span), 0)
+    factor = size ** (-0.5) * LOG2E
+    halves, sums = [], []
+    for h in range(2):
+        mine = lane < size if h == 0 else lane >= size
+        other = (1 - h) * size
+        qh = jnp.where(mine, q, jnp.where(lane == other, 1.0, 0.0).astype(BF16))
+        kh = jnp.where(mine, k, fill)
+        scores = nt(kh, qh)
+        top = jnp.max(scores, axis=0, keepdims=True)
+        e = jnp.exp2((scores - top) * factor).astype(BF16)
+        vmine = vrow < size if h == 0 else vrow >= size
+        vh = jnp.where(vmine, vt, jnp.ones_like(vt))
+        o = nn(vh, e)
+        total = o[other : other + 1, :]
+        halves.append(o[h * size : (h + 1) * size, :] / total)
+        sums.append(top * factor + jnp.log2(total))
+    ct = jnp.concatenate(halves, axis=0)
+    ctx[rows, pl.ds(pl.multiple_of(hp * wide, wide), wide)] = ct.T.astype(BF16)
+    lse[i] = jnp.concatenate(sums + [jnp.zeros((6, span), F32)], axis=0)
+
+
+class Gather:
+    def __init__(self, buf, send, recv, split):
+        self.buf, self.send, self.recv = buf, send, recv
+        self.nz, _, self.r, self.cols = buf.shape
+        self.x, self.c, self.z, self.y = here()
+        self.half = self.cols // 2
+        self.split = split
+        self.base = {"z": 0}
+        total = 0
+        for kind, count in (("z", self.nz), ("xo", self.nz), ("ya1", self.nz), ("ya2", self.nz), ("xa", self.nz), ("co", self.nz), ("cx", self.nz)):
+            self.base[kind] = total
+            total += count
+
+    def region(self, kind, k, sender):
+        x, c, z, y = sender
+        zk = lax.rem(self.z + self.nz - k, self.nz)
+        if kind == "z":
+            zk = z
+        row = pl.ds(pl.multiple_of(x * (self.r // 2), 16), self.r // 2)
+        every = pl.ds(0, self.r)
+        c0 = c * self.half
+        first = pl.ds(pl.multiple_of(c0, 128), self.split)
+        second = pl.ds(pl.multiple_of(c0 + self.split, 128), self.half - self.split)
+        both = pl.ds(pl.multiple_of(c0, 128), self.half)
+        yy, rr, cc = {
+            "z": (y, row, both),
+            "xo": (y, row, both),
+            "ya1": (y, every, first),
+            "ya2": (y, row, second),
+            "xa": (1 - y, row, second),
+            "co": (y, every, both),
+            "cx": (1 - y, every, both),
+        }[kind]
+        return self.buf.at[zk, yy, rr, cc]
+
+    def peer(self, kind, k):
+        x, c, z, y = self.x, self.c, self.z, self.y
+        if kind == "z":
+            return x, c, lax.rem(z + k, self.nz), y
+        if kind in ("xo", "xa"):
+            return 1 - x, c, z, y
+        if kind in ("ya1", "ya2"):
+            return x, c, z, 1 - y
+        return x, 1 - c, z, y
+
+    def copy(self, kind, k, incoming):
+        me = (self.x, self.c, self.z, self.y)
+        peer = self.peer(kind, k)
+        sender = me
+        if incoming:
+            sender = (self.x, self.c, lax.rem(self.z + self.nz - k, self.nz), self.y) if kind == "z" else peer
+        ref = self.region(kind, k, sender)
+        n = self.base[kind] + k
+        return pltpu.make_async_remote_copy(
+            src_ref=ref, dst_ref=ref, send_sem=self.send.at[n], recv_sem=self.recv.at[n], device_id=at(*peer), device_id_type=MESH
+        )
+
+    def go(self, kind, k):
+        self.copy(kind, k, False).start()
+
+    def got(self, kind, k):
+        self.copy(kind, k, True).wait_recv()
+
+    def start_z(self):
+        for k in range(1, self.nz):
+            self.go("z", k)
+
+    def steps(self):
+        out = []
+        ks = range(1, self.nz)
+
+        def s0():
+            self.go("ya1", 0)
+            self.go("ya2", 0)
+
+        out.append(s0)
+
+        def s1(k):
+            self.got("z", k)
+            self.go("xo", k)
+            self.go("ya2", k)
+
+        for k in ks:
+            out.append(functools.partial(s1, k))
+
+        def s2():
+            self.got("ya2", 0)
+            self.go("xa", 0)
+
+        out.append(s2)
+
+        def s3(k):
+            self.got("xo", k)
+            self.go("ya1", k)
+            self.go("co", k)
+            self.got("ya2", k)
+            self.go("xa", k)
+
+        for k in ks:
+            out.append(functools.partial(s3, k))
+
+        def s4(k):
+            self.got("ya1", k)
+            self.got("xa", k)
+            self.go("cx", k)
+
+        for k in range(self.nz):
+            out.append(functools.partial(s4, k))
+        return out
+
+    def finish(self):
+        for k in range(1, self.nz):
+            self.got("co", k)
+        for k in range(self.nz):
+            self.got("cx", k)
+
+    def drain(self):
+        for kind in ("z", "xo", "ya1", "ya2", "xa", "co", "cx"):
+            for k in range(self.nz):
+                if k == 0 and kind in ("z", "xo", "co"):
+                    continue
+                self.copy(kind, k, False).wait_send()
+
+
+def gelu_both(value):
+    cdf = 0.5 + 0.5 * lax.erf(value * (0.5**0.5))
+    bell = jnp.exp2(value * value * (-0.5 * LOG2E)) * (1.0 / math.sqrt(2.0 * math.pi))
+    return value * cdf, cdf + value * bell
+
+
+def place(sm, f, part, width):
+    row = lax.broadcasted_iota(jnp.int32, (128, width), 0)
+    col = lax.broadcasted_iota(jnp.int32, (128, width), 1)
+    return jnp.where((col == row + f * part) & (row < part), 1.0, 0.0).astype(BF16)
+
+
+def forward_kernel(comm, tokens_h, lengths, wqkv_h, wout_h, winner_h, wouter_h, wpool_h, smalls_h,
+                   out_h, w1_h, w2_h, w3_h, vec_o, ib_o, qkv_h, ctx_h, lse_o, hid_h, u1_h, act_h, dg_h, u2_h, inv_o, first_o,
+                   tokens, w1, w2, w3, sm, qkv, ctx, hid, hidlow, u1, act, dg, u2, outv,
+                   loc, s_sm, r_sm, s1, r1, s2, r2, s3, r3):
+    x, c, z, y = here() if comm else (0, 0, 0, 0)
+    nz = w1.shape[0]
+    rows, width = tokens.shape
+    span = rows // lengths.shape[0]
+    ff = act.shape[1]
+    size = width // HEADS
+    pairs = HEADS // 2
+    d3 = 3 * width
+    fr = wouter_h.shape[0] if comm else w3.shape[2] - w1.shape[2]
+
+    if comm:
+        barrier = pltpu.get_barrier_semaphore()
+        peers = [(x, c, lax.rem(z + k, nz), yy) for k in range(1, nz) for yy in (y, 1 - y)]
+        peers += [(x, c, z, 1 - y), (1 - x, c, z, y), (x, 1 - c, z, y)]
+        local = []
+
+        def bring(n, src, dst):
+            copy = pltpu.make_async_copy(src, dst, loc.at[n])
+            copy.start()
+            local.append(copy)
+
+        f_me = z * 2 + y
+        bring(0, wqkv_h, w1.at[z, y])
+        bring(1, smalls_h, sm.at[f_me])
+        bring(2, wout_h, w2.at[z, y, :, pl.ds(0, width)])
+        bring(3, winner_h, w2.at[z, y, :, pl.ds(width, ff)])
+        bring(4, wouter_h, w3.at[z, y, pl.ds(0, fr)])
+        bring(5, wpool_h, w3.at[z, y, pl.ds(fr, wpool_h.shape[0])])
+        bring(6, tokens_h, tokens)
+        for p in peers:
+            pl.semaphore_signal(barrier, inc=1, device_id=at(*p), device_id_type=MESH)
+        pl.semaphore_wait(barrier, len(peers))
+        g1 = Gather(w1, s1, r1, 512)
+        g2 = Gather(w2, s2, r2, 640)
+        g3 = Gather(w3, s3, r3, 128)
+        local[0].wait()
+        g1.start_z()
+        local[1].wait()
+        others = [p for p in peers[:-2]]
+
+        def small(n, slot):
+            px, pc, pz, py = others[n]
+            return pltpu.make_async_remote_copy(
+                src_ref=sm.at[slot], dst_ref=sm.at[slot], send_sem=s_sm.at[n], recv_sem=r_sm.at[n], device_id=at(px, pc, pz, py), device_id_type=MESH
+            )
+
+        for n in range(len(others)):
+            small(n, f_me).start()
+        todo = g1.steps()
+        for n, step in enumerate(todo):
+            step()
+            if n == 4:
+                local[2].wait()
+                local[3].wait()
+                g2.start_z()
+        local[4].wait()
+        local[5].wait()
+        g3.start_z()
+        for n in range(len(others)):
+            if n < 2 * (nz - 1):
+                k, same = n // 2 + 1, n % 2 == 0
+                slot = lax.rem(z + nz - k, nz) * 2 + (y if same else 1 - y)
+            else:
+                slot = z * 2 + 1 - y
+            small(n, slot).wait_recv()
+        local[6].wait()
+        g1.finish()
+        steps2, steps3 = g2.steps(), g3.steps()
+    else:
+        steps2, steps3 = [], []
+        for n, (a, b) in enumerate(((tokens_h, tokens), (w1_h, w1), (w2_h, w2), (w3_h, w3), (smalls_h, sm))):
+            cp = pltpu.make_async_copy(a, b, loc.at[n])
+            cp.start()
+            cp.wait()
+
+    nf = nz * 2
+    part = width // nf
+    vec = jnp.zeros((sm.shape[1], width), F32)
+    for f in range(nf):
+        vec += nn(sm[f], place(None, f, part, width))
+    vec_o[...] = vec
+    ibs = []
+    for f in range(nf):
+        piece = sm[f].astype(F32)
+        for j in range(ff // nf // 128):
+            ibs.append(piece[12 + j : 13 + j, :])
+    ib_o[...] = jnp.broadcast_to(jnp.concatenate(ibs, axis=1), ib_o.shape)
+
+    out_copies = []
+
+    def save(src, dst):
+        cp = pltpu.make_async_copy(src, dst, loc.at[8 + len(out_copies)])
+        cp.start()
+        out_copies.append(cp)
+
+    if comm:
+        save(w1, w1_h)
+
+    tile = 256
+    zero_row = jnp.zeros((1, width), F32)
+    biases = (vec_o[0:1, :], zero_row, vec_o[1:2, :])
+
+    def project(i, _):
+        r = pl.ds(pl.multiple_of(i * tile, tile), tile)
+        t = tokens[r, :]
+        for p in range(3):
+            w = w1[:, :, :, p * width : (p + 1) * width].reshape(width, width)
+            qkv[r, p * width : (p + 1) * width] = (nn(t, w) + biases[p]).astype(BF16)
+        for n, step in enumerate(steps2[:4]):
+            pl.when(i == n)(step)
+        return 0
+
+    lax.fori_loop(0, rows // tile, project, 0)
+    save(qkv, qkv_h)
+
+    def attention(i, _):
+        attend_forward(qkv, ctx, lse_o, lengths, i, span, width, size)
+        for n, step in enumerate(steps2[4:]):
+            pl.when(i == n)(step)
+        for n, step in enumerate(steps3[:4]):
+            pl.when(i == n + 8)(step)
+        return 0
+
+    lax.fori_loop(0, (rows // span) * pairs, attention, 0)
+    save(ctx, ctx_h)
+    if comm:
+        g2.finish()
+        save(w2, w2_h)
+
+    b_out, g_first, s_first, b_outer, g_second, s_second = (vec_o[n : n + 1, :] for n in range(2, 8))
+
+    def stage_one(i, _):
+        r = pl.ds(pl.multiple_of(i * tile, tile), tile)
+        w = w2[:, :, :, :width].reshape(width, width)
+        resid = tokens[r, :].astype(F32) + (nn(ctx[r, :], w) + b_out)
+        centred = resid - rowmean(resid)
+        inv = lax.rsqrt(rowmean(centred * centred) + EPS)
+        unit = centred * inv
+        u1[r, :] = unit.astype(BF16)
+        inv_o[0, r, :] = jnp.broadcast_to(inv, (tile, 128))
+        h = unit * g_first + s_first
+        hid[r, :] = h
+        low = h.astype(BF16)
+        hidlow[r, :] = low
+        for b in range(ff // width):
+            cols = pl.ds(b * width, width)
+            w = w2[:, :, :, (b + 1) * width : (b + 2) * width].reshape(width, width)
+            a, g = gelu_both(nn(low, w) + ib_o[0:1, b * width : (b + 1) * width])
+            act[r, cols] = a.astype(BF16)
+            dg[r, cols] = g.astype(BF16)
+        for n in range(rows // tile):
+            for step in steps3[4 + 2 * n : 6 + 2 * n]:
+                pl.when(i == n)(step)
+        return 0
+
+    lax.fori_loop(0, rows // tile, stage_one, 0)
+    save(u1, u1_h)
+    save(hidlow, hid_h)
+    save(act, act_h)
+    save(dg, dg_h)
+    if comm:
+        g3.finish()
+        save(w3, w3_h)
+
+    def stage_two(i, _):
+        r = pl.ds(pl.multiple_of(i * tile, tile), tile)
+        w = w3[:, :, :fr, :].reshape(ff, width)
+        resid = hid[r, :] + (nn(act[r, :], w) + b_outer)
+        centred = resid - rowmean(resid)
+        inv = lax.rsqrt(rowmean(centred * centred) + EPS)
+        unit = centred * inv
+        u2[r, :] = unit.astype(BF16)
+        inv_o[1, r, :] = jnp.broadcast_to(inv, (tile, 128))
+        layer = unit * g_second + s_second
+        each = span // tile
+        s, j = i // each, i % each
+
+        @pl.when(j == 0)
+        def _():
+            first_o[pl.ds(pl.multiple_of(s * 8, 8), 8), :] = layer[0:8, :]
+
+        slot = lax.broadcasted_iota(jnp.int32, (tile, width), 0) + j * tile
+        outv[r, :] = jnp.where(slot < lengths[s], layer, 0.0).astype(BF16)
+        return 0
+
+    lax.fori_loop(0, rows // tile, stage_two, 0)
+    save(u2, u2_h)
+    save(outv, out_h)
+    for cp in out_copies:
+        cp.wait()
+    if comm:
+        for n in range(len(others)):
+            small(n, f_me).wait_send()
+        for g in (g1, g2, g3):
+            g.drain()
+
+
+def forward(tokens, lengths, wqkv, wout, winner, wouter, wpool, smalls, nz, gathered=None):
+    rows, width = tokens.shape
+    comm = gathered is None
+    span = rows // lengths.shape[0]
+    nf = nz * 2
+    ff = winner.shape[1] if comm else gathered[1].shape[3] - width
+    part = width // nf
+    fpart = ff // nf
+    any_, vm, smem = (pl.BlockSpec(memory_space=m) for m in (pl.ANY, pltpu.VMEM, pltpu.SMEM))
+    S = jax.ShapeDtypeStruct
+    pairs = HEADS // 2
+    outs = [
+        (S((rows, width), BF16), any_),
+        (S((nz, 2, part, 3 * width), BF16), any_),
+        (S((nz, 2, part, width + ff), BF16), any_),
+        (S((nz, 2, fpart + part, width), BF16), any_),
+        (S((16, width), F32), vm),
+        (S((8, ff), F32), vm),
+        (S((rows, 3 * width), BF16), any_),
+        (S((rows, width), BF16), any_),
+        (S(((rows // span) * pairs, 8, span), F32), vm),
+        (S((rows, width), BF16), any_),
+        (S((rows, width), BF16), any_),
+        (S((rows, ff), BF16), any_),
+        (S((rows, ff), BF16), any_),
+        (S((rows, width), BF16), any_),
+        (S((2, rows, 128), F32), vm),
+        (S((8 * (rows // span), width), F32), vm),
+    ]
+    V = pltpu.VMEM
+    D = pltpu.SemaphoreType.DMA
+    scratch = [
+        V((rows, width), BF16),
+        V((nz, 2, part, 3 * width), BF16),
+        V((nz, 2, part, width + ff), BF16),
+        V((nz, 2, fpart + part, width), BF16),
+        V((nf, 16, 128), BF16),
+        V((rows, 3 * width), BF16),
+        V((rows, width), BF16),
+        V((rows, width), F32),
+        V((rows, width), BF16),
+        V((rows, width), BF16),
+        V((rows, ff), BF16),
+        V((rows, ff), BF16),
+        V((rows, width), BF16),
+        V((rows, width), BF16),
+        D((24,)), D((nf,)), D((nf,)),
+        D((7 * nz,)), D((7 * nz,)), D((7 * nz,)), D((7 * nz,)), D((7 * nz,)), D((7 * nz,)),
+    ]
+    kern = functools.partial(forward_kernel, comm)
+    params = pltpu.CompilerParams(vmem_limit_bytes=60 * 2**20, has_side_effects=True, **({"collective_id": 0} if comm else {}))
+    flops = 2 * rows * width * (4 * width + 2 * ff)
+    cost = pl.CostEstimate(flops=flops, bytes_accessed=10**7, transcendentals=0)
+    if comm:
+        args = (tokens, lengths, wqkv, wout, winner, wouter, wpool, smalls)
+        return pl.pallas_call(kern, out_shape=[o[0] for o in outs], out_specs=[o[1] for o in outs],
+                              in_specs=[any_, smem] + [any_] * 6, scratch_shapes=scratch, compiler_params=params, cost_estimate=cost)(*args)
+
+    def solo(tokens_h, lengths, w1_h, w2_h, w3_h, smalls_h, *rest):
+        o = rest[: len(outs)]
+        forward_kernel(False, tokens_h, lengths, None, None, None, None, None, smalls_h, o[0], w1_h, w2_h, w3_h, *o[4:], *rest[len(outs):])
+
+    return pl.pallas_call(solo, out_shape=[o[0] for o in outs], out_specs=[o[1] for o in outs],
+                          in_specs=[any_, smem] + [any_] * 4, scratch_shapes=scratch, compiler_params=params, cost_estimate=cost)(
+        tokens, lengths, *gathered, smalls)
 
 
 def normalize(value, gain, shift):
@@ -29,7 +501,7 @@
 
 
 def matmul(left, right):
-    return jnp.dot(left, right, preferred_element_type=jnp.float32)
+    return nn(left, right)
 
 
 def transposed_left(left, right):
@@ -86,7 +558,7 @@
     )
 
 
-def per_device(
+def per_device_any(
     tokens,
     lengths,
     labels,
@@ -326,6 +798,156 @@
     )
 
 
+def per_device(nz, tokens, lengths, labels, cotangent, qkv_weight, query_bias, value_bias, out_weight, out_bias,
+    first_gain, first_shift, inner_weight, inner_bias, outer_weight, outer_bias, second_gain, second_shift,
+    pool_weight, pool_bias, class_weight, class_bias):
+    part = query_bias.shape[0]
+    vectors = jnp.stack([query_bias, value_bias, out_bias, first_gain, first_shift, outer_bias, second_gain, second_shift, pool_bias]
+                        + [class_weight[:, j] for j in range(class_weight.shape[1])])
+    smalls = jnp.concatenate([jnp.pad(vectors, ((0, 0), (0, 128 - part))), inner_bias.reshape(-1, 128), jnp.zeros((1, 128), BF16)])
+    (output, w1, w2, w3, vec, ib, qkv, context, lse, hidden_low, unit_first, act, dgelu, unit_second, inv, firsts) = forward(
+        tokens, lengths, qkv_weight, out_weight, inner_weight, outer_weight, pool_weight, smalls, nz)
+    seqs = lengths.shape[0]
+    rows, width = tokens.shape
+    ff = act.shape[1]
+    span = rows // seqs
+    size = width // HEADS
+    classes = class_bias.shape[0]
+    w_qkv = w1.reshape(width, 3 * width)
+    w2 = w2.reshape(width, width + ff)
+    w_out, w_inner = w2[:, :width], w2[:, width:]
+    fr = ff // (2 * nz)
+    w_outer = w3[:, :, :fr].reshape(ff, width)
+    w_pool = w3[:, :, fr:].reshape(width, width)
+    g_first, g_second, b_pool, w_class = vec[3], vec[6], vec[8], vec[9:12].T.astype(BF16)
+    b_class = class_bias.astype(jnp.float32)
+    unit_first, unit_second = unit_first.astype(F32), unit_second.astype(F32)
+    inverse_first, inverse_second = inv[0, :, :1], inv[1, :, :1]
+    position = lax.broadcasted_iota(jnp.int32, (seqs, span), 1)
+    keep = position < lengths[:, None]
+    valid = keep.reshape(rows, 1).astype(jnp.float32)
+    query = qkv[:, :width].reshape(seqs, span, HEADS, size)
+    key = qkv[:, width : 2 * width].reshape(seqs, span, HEADS, size)
+    value = qkv[:, 2 * width :].reshape(seqs, span, HEADS, size)
+    logsum = (lse[:, :2] / LOG2E).reshape(seqs, HEADS, span)
+    first = firsts[::8].astype(BF16)
+    pooled = jnp.tanh(matmul(first, w_pool) + b_pool)
+    pooled_low = pooled.astype(jnp.bfloat16)
+    logits = matmul(pooled_low, w_class) + b_class
+    peak = jnp.max(logits, axis=-1, keepdims=True)
+    logsum_class = peak + jnp.log(jnp.sum(jnp.exp(logits - peak), axis=-1, keepdims=True))
+    onehot = (labels[:, None] == lax.broadcasted_iota(jnp.int32, (seqs, classes), 1)).astype(
+        jnp.float32
+    )
+    exit_loss = logsum_class[:, 0] - jnp.sum(onehot * logits, axis=-1)
+    grad_logits = (jnp.exp(logits - logsum_class) - onehot).astype(jnp.bfloat16)
+    grad_class_weight = transposed_left(pooled_low, grad_logits)
+    grad_class_local = column_sum(grad_logits)
+    grad_pooled = transposed_right(grad_logits, w_class)
+    grad_pre = (grad_pooled * (1.0 - pooled * pooled)).astype(jnp.bfloat16)
+    grad_pool_weight = transposed_left(first, grad_pre)
+    grad_pool_bias = column_sum(grad_pre)
+    grad_first = transposed_right(grad_pre, w_pool)
+    grad_layer = (cotangent.astype(jnp.float32) * valid).reshape(seqs, span, width)
+    grad_layer = jnp.concatenate(
+        [grad_layer[:, :1] + grad_first[:, None, :], grad_layer[:, 1:]], axis=1
+    )
+    grad_layer = grad_layer.reshape(rows, width)
+    grad_resid_second, grad_second_gain, grad_second_shift = norm_back(
+        grad_layer, unit_second, inverse_second, g_second
+    )
+    grad_ffn = grad_resid_second.astype(jnp.bfloat16)
+    grad_outer_weight = transposed_left(act, grad_ffn)
+    grad_outer_bias = column_sum(grad_ffn)
+    grad_act = transposed_right(grad_ffn, w_outer)
+    grad_inner = (grad_act * dgelu.astype(F32)).astype(jnp.bfloat16)
+    grad_inner_weight = transposed_left(hidden_low, grad_inner)
+    grad_inner_bias = column_sum(grad_inner)
+    grad_hidden = grad_resid_second + transposed_right(grad_inner, w_inner)
+    grad_resid_first, grad_first_gain, grad_first_shift = norm_back(
+        grad_hidden, unit_first, inverse_first, g_first
+    )
+    grad_attended = grad_resid_first.astype(jnp.bfloat16)
+    grad_out_weight = transposed_left(context, grad_attended)
+    grad_out_bias = column_sum(grad_attended)
+    grad_context = (
+        transposed_right(grad_attended, w_out).astype(jnp.bfloat16).reshape(seqs, span, HEADS, size)
+    )
+    grad_query, grad_key, grad_value = lax.map(
+        attend_back, (query, key, value, keep, logsum, grad_context)
+    )
+    grad_query = grad_query.reshape(rows, width)
+    grad_key = grad_key.reshape(rows, width)
+    grad_value = grad_value.reshape(rows, width)
+    grad_qkv = jnp.concatenate([grad_query, grad_key, grad_value], axis=1)
+    grad_qkv_weight = transposed_left(tokens, grad_qkv)
+    grad_query_bias = column_sum(grad_query)
+    grad_value_bias = column_sum(grad_value)
+    tokens_grad = (grad_resid_first + transposed_right(grad_qkv, w_qkv)).astype(jnp.bfloat16)
+    owned = (
+        lax.psum_scatter(grad_qkv_weight, "fsdp", scatter_dimension=0, tiled=True),
+        lax.psum_scatter(grad_query_bias, "fsdp", scatter_dimension=0, tiled=True),
+        lax.psum_scatter(grad_value_bias, "fsdp", scatter_dimension=0, tiled=True),
+        lax.psum_scatter(grad_out_weight, "fsdp", scatter_dimension=0, tiled=True),
+        lax.psum_scatter(grad_out_bias, "fsdp", scatter_dimension=0, tiled=True),
+        lax.psum_scatter(grad_first_gain, "fsdp", scatter_dimension=0, tiled=True),
+        lax.psum_scatter(grad_first_shift, "fsdp", scatter_dimension=0, tiled=True),
+        lax.psum_scatter(grad_inner_weight, "fsdp", scatter_dimension=0, tiled=True),
+        lax.psum_scatter(grad_inner_bias, "fsdp", scatter_dimension=0, tiled=True),
+        lax.psum_scatter(grad_outer_weight, "fsdp", scatter_dimension=0, tiled=True),
+        lax.psum_scatter(grad_outer_bias, "fsdp", scatter_dimension=0, tiled=True),
+        lax.psum_scatter(grad_second_gain, "fsdp", scatter_dimension=0, tiled=True),
+        lax.psum_scatter(grad_second_shift, "fsdp", scatter_dimension=0, tiled=True),
+        lax.psum_scatter(grad_pool_weight, "fsdp", scatter_dimension=0, tiled=True),
+        lax.psum_scatter(grad_pool_bias, "fsdp", scatter_dimension=0, tiled=True),
+        lax.psum_scatter(grad_class_weight, "fsdp", scatter_dimension=0, tiled=True),
+    )
+    summed = lax.psum(
+        (
+            owned[0],
+            owned[1],
+            owned[2],
+            owned[3],
+            owned[4],
+            owned[5],
+            owned[6],
+            owned[7],
+            owned[8],
+            owned[9],
+            owned[10],
+            owned[11],
+            owned[12],
+            owned[13],
+            owned[14],
+            owned[15],
+        ),
+        "dp",
+    )
+    class_bias_grad = lax.psum(grad_class_local, ("dp", "fsdp"))
+    return (
+        output,
+        exit_loss,
+        tokens_grad,
+        summed[0],
+        summed[1],
+        summed[2],
+        summed[3],
+        summed[4],
+        summed[5],
+        summed[6],
+        summed[7],
+        summed[8],
+        summed[9],
+        summed[10],
+        summed[11],
+        summed[12],
+        summed[13],
+        summed[14],
+        summed[15],
+        class_bias_grad,
+    )
+
+
 def solution(mesh):
     in_specs = (
         P(("dp", "fsdp"), None),
@@ -372,6 +994,8 @@
         P("fsdp", None),
         P(),
     )
+    sizes = dict(mesh.shape)
+    fast = sizes["dp"] == 4 and sizes["fsdp"] == 8
     return jax.shard_map(
-        per_device, mesh=mesh, in_specs=in_specs, out_specs=out_specs, check_vma=False
-    )
+        functools.partial(per_device, sizes["fsdp"] // 2) if fast else per_device_any, mesh=mesh, in_specs=in_specs, out_specs=out_specs, check_vma=False
+    )

time: 1230 us -> 1040 us (0.85)
  Pallas kernels: 0 us -> 94.4 us
  waiting for transfers between devices: 726 us -> 633 us
  blocking collectives: 167 us -> 84.9 us
  matrix products: 180 us -> 100 us
  other arithmetic: 40.9 us -> 26.9 us
  local copies, waits for them, and re-layouts: 90.8 us -> 76.8 us
    all_gather x5 -> x0, waiting for transfers between devices: 99.7 us -> none  [the longest x1 44.3 us: per_device(): lax.all_gather(outer_weight, 'fsdp', axis=0, tiled=True)]
    pallas_call x0 -> x1, Pallas kernels: none -> 94.4 us  [forward(): pl.pallas_call(kern, out_shape=[o[0] for o in outs], out_specs=[o[1] for...]
    dot_general x10 -> x2, matrix products: 70.8 us -> 1.79 us  [nn(): return jnp.dot(left, right, preferred_element_type=F32)]
    all_gather x2 -> x0, blocking collectives: 42.7 us -> none  [the longest x1 26.2 us: per_device(): lax.all_gather(inner_bias, 'fsdp', axis=0, tiled=True)]
    unnamed x2 -> x1, blocking collectives: 77.4 us -> 37.6 us
    unnamed x165 -> x129, local copies, waits for them, and re-layouts: 43.1 us -> 27.7 us
    unnamed x14 -> x9, waiting for transfers between devices: 97.4 us -> 105 us
  transfers between devices with their start and end apart: 12 -> 7, of which waited for: 9 -> 6; matrix products, arithmetic and copies ran while one was open for 14% -> 4% of each run, Pallas kernels for 0% -> 0%
where the time goes in v1:
time: 1040 us; the launch traced here: 1030 us
  waiting for transfers between devices  633 us (61%)
  matrix products  100 us (10%)
  Pallas kernels  94.4 us (9%)
  blocking collectives  84.9 us (8%)
  local copies, waits for them, and re-layouts  76.8 us (7%)
  other arithmetic  26.9 us (3%)
  between operations  16.5 us (2%)
    reduce_scatter x1, waiting for transfers between devices, per_device(): lax.psum_scatter(grad_inner_weight, 'fsdp', scatter_dimension=0, tiled=True)  166 us
    reduce_scatter x1, waiting for transfers between devices, per_device(): lax.psum_scatter(grad_outer_weight, 'fsdp', scatter_dimension=0, tiled=True)  166 us
    unnamed x9, waiting for transfers between devices  105 us
    pallas_call x1, Pallas kernels, forward(): pl.pallas_call(kern, out_shape=[o[0] for o in outs], out_specs=[o[1] for...  94.4 us
    reduce_scatter x1, waiting for transfers between devices, per_device(): lax.psum_scatter(grad_out_weight, 'fsdp', scatter_dimension=0, tiled=True)  72 us
    reduce_scatter x1, waiting for transfers between devices, per_device(): lax.psum_scatter(grad_pool_weight, 'fsdp', scatter_dimension=0, tiled=True)  69.5 us
    psum x1, waiting for transfers between devices, per_device(): lax.psum((owned[0], owned[1], owned[2], owned[3], owned[4], owned[5], own...  53.9 us
    psum x1, blocking collectives, per_device(): class_bias_grad = lax.psum(grad_class_local, ('dp', 'fsdp'))  39.5 us
  transfers between devices with their start and end apart: 7, of which 6 were waited for; matrix products, arithmetic and copies ran while one was open for 4% of the time, Pallas kernels for 0%

profile of v1, /device:TPU:0, one launch (start us, length us, event | category | flops | bytes accessed | tf_op | source)
XLA Modules:
  0.0 1033.9 jit_solution(5036724142849210894)
XLA Ops:
  11.9 94.4 %shard_map.356 = (bf16[1024,768]{1,0:T(8,128)(2,1)}, bf16[4,2,96,2304]{3,2,1,0:T(8,128)(2,1)}, bf16[4,2,96,3840]{3,2,1,0:T(8,128)(2,1)}, bf16[4,2,480,768]{3,2,1...) custom-call(bf16[1024,768]{1,0:T(8,128)(2,1)} %tokens_h.1, ...), custom_call_target="tpu_custom_call" | custom-call | flops 14495514624 | bytes 10000000 | tf_op jit(solution)/shard_map/pallas_call | solution.py:473
  108.6 4.8 slice.73
  127.0 10.7 %convert_reduce_fusion = (f32[3072]{0:T(1024)}, bf16[1024,3072]{1,0:T(8,128)(2,1)}) fusion(bf16[1024,3072]{1,0:T(8,128)(2,1)} %get-tuple-element.95, bf16[3072,768]{1,0:T(8,128)(2,1)S(1)} %bitcast.168, f32[1024,768]{1,0:T(8,128)S(1)} %get-tuple-element.259), kind=kOutput, calls=%fused_computation.40 | convolution fusion | flops 4848350208 | bytes 20459520 | tf_op jit(solution)/shard_map/dot_general | solution.py:514
  137.8 8.8 fusion.49
  182.4 48.5 %while.14 = (s32[]{:T(128)}, bf16[2,512,12,64]{1,3,2,0:T(8,128)(2,1)}, bf16[2,512,12,64]{1,3,2,0:T(8,128)(2,1)}, bf16[2,512,12,64]{1,3,2,0:T(8,128)(2,1)}, bf16[...) while((s32[]{:T(128)}, ...), condition=%wide.region_9.10_spmd, body=%wide.region_7.0_spmd.sunk | while | flops 2062411776 | bytes 152764272 | solution.py:876
  187.8 7.3 multiply_reduce_fusion.4
  195.2 7.2 multiply_convert_fusion.5
  211.8 7.3 multiply_reduce_fusion.4
  219.1 7.2 multiply_convert_fusion.5
  241.1 5.8 convolution_bitcast_fusion
  246.9 8.0 copy.87
  257.6 5.2 fusion.63
  262.9 10.6 %fusion.66 = f32[3072,768]{1,0:T(8,128)} fusion(bf16[1024,3072]{1,0:T(8,128)(2,1)} %get-tuple-element.106, f32[1024,768]{1,0:T(8,128)} %copy-done.10), kind=kOutput, calls=%fused_computation.115 | convolution fusion | flops 4832624640 | bytes 18874368 | tf_op jit(solution)/shard_map/dot_general | solution.py:508
  273.6 9.8 fusion.75
  285.2 104.4 %reduce-scatter.19.cloned.1.call-done = f32[96,2304]{1,0:T(8,128)} async-done(((f32[768,2304]{1,0:T(8,128)}), f32[96,2304]{1,0:T(8,128)}) %reduce-scatter.19.cloned.1.call-update) | async-done | bytes 884752
  392.2 69.5 %reduce-scatter.17.cloned.1.call-done = f32[96,768]{1,0:T(8,128)} async-done(((f32[768,768]{1,0:T(8,128)}), f32[96,768]{1,0:T(8,128)}) %reduce-scatter.17.cloned.1.call-update) | async-done | bytes 294928 | tf_op jit(solution)/shard_map/reduce_scatter | solution.py:901
  461.7 72.0 %reduce-scatter.11.cloned.1.call-done = f32[96,768]{1,0:T(8,128)} async-done(((f32[768,768]{1,0:T(8,128)}), f32[96,768]{1,0:T(8,128)}) %reduce-scatter.11.cloned.1.call-update) | async-done | bytes 294928 | tf_op jit(solution)/shard_map/reduce_scatter | solution.py:891
  533.7 166.4 %reduce-scatter.15.cloned.1.call-done = f32[384,768]{1,0:T(8,128)} async-done(((f32[3072,768]{1,0:T(8,128)}), f32[384,768]{1,0:T(8,128)}) %reduce-scatter.15.cloned.1.call-update) | async-done | bytes 1179664 | tf_op jit(solution)/shard_map/reduce_scatter | solution.py:897
  700.1 166.5 %reduce-scatter.13.cloned.1.call-done = f32[96,3072]{1,0:T(8,128)} async-done(((f32[768,3072]{1,0:T(8,128)}), f32[96,3072]{1,0:T(8,128)}) %reduce-scatter.13.cloned.1.call-update) | async-done | bytes 1179664 | tf_op jit(solution)/shard_map/reduce_scatter | solution.py:895
  866.7 39.5 %psum.135 = f32[3]{0:T(128)} all-reduce(f32[3]{0:T(128)S(1)} %copy-done.51), channel_id=1, replica_groups=mesh['dp'=4,'fsdp'=8] {'dp','fsdp'}, use_global_device_ids=true, to_apply=%region_54.55 | all-reduce | flops 3 | bytes 24 | tf_op jit(solution)/shard_map/psum | solution.py:926
  908.9 37.6 %all-reduce.11 = (f32[768]{0:T(1024)S(1)}, f32[768]{0:T(1024)S(1)}, f32[768]{0:T(1024)S(1)}, f32[768]{0:T(1024)S(1)}, f32[768]{0:T(1024)S(1)}, /*index=5*/f32[30...) all-reduce(f32[768]{0:T(1024)S(1)} %reduce_sum.181, ...), channel_id=3, replica_groups=mesh['dp'=4,'fsdp'=8] {'fsdp'}, use_global_device_ids=true, to_apply=%region_13.14.clone | all-reduce | flops 9984 | bytes 79872
  947.3 9.4 add_convert_fusion
  957.7 7.8 all-reduce.12
  965.5 53.9 %all-reduce.16.cloned.1.call-done = (f32[96,2304]{0,1:T(8,128)}, f32[96,768]{1,0:T(8,128)}, f32[96,3072]{1,0:T(8,128)}, f32[384,768]{1,0:T(8,128)}, f32[96,768]{1,0:T(8,128)}) async-done(((f32[96,2304]{0,1:T(8,128)}, f32[96,768]{1,0:T(8,128)}, f32[96,3072]{1,0:T(8,128)}, f32[384,768]{1,0:T(8,128)}, f32[96,768]{1,0:T(8,128)}), (f32[96,2304]{0,1:T(8,128)}, f32[96,768]{1,0:T(8,128)}, f32[96,3072]{1,0:T(8,128)}, ...) | async-done | bytes 3833872 | tf_op jit(solution)/shard_map/psum | solution.py:905
  (248 shorter events, 102.1 us)
Async XLA Ops:
  7.2 382.5 %reduce-scatter.19.cloned.1.call-start = ((), (), s32[]{:S(2)}) async-start(), calls=%async_computation.10 | async-start | bytes 7962624
  108.6 9.3 copy-start.40
  125.2 12.6 %slice-start.2 = ((s8[5898240]{0:T(1024)(128)(4,1)}), s8[4194304]{0:T(1024)(128)(4,1)S(1)}, s32[]{:S(2)}) async-start(s8[5898240]{0:T(1024)(128)(4,1)} %bitcast.181), calls=%async_computation.15 | async-start | bytes 8388608
  127.0 10.8 %copy-start.10 = (f32[1024,768]{1,0:T(8,128)}, f32[1024,768]{1,0:T(8,128)S(1)}, u32[]{:S(2)}) copy-start(f32[1024,768]{1,0:T(8,128)S(1)} %get-tuple-element.259) | copy-start | bytes 9437188
  127.0 10.8 %copy-start.11 = (bf16[1024,768]{1,0:T(8,128)(2,1)S(1)}, bf16[1024,768]{1,0:T(8,128)(2,1)}, u32[]{:S(2)}) copy-start(bf16[1024,768]{1,0:T(8,128)(2,1)} %get-tuple-element.97) | copy-start | bytes 4718596
  127.0 10.8 %slice-start.3 = ((s8[5898240]{0:T(1024)(128)(4,1)}), s8[1703936]{0:T(1024)(128)(4,1)S(1)}, s32[]{:S(2)}) async-start(s8[5898240]{0:T(1024)(128)(4,1)} %bitcast.181), calls=%async_computation.16 | async-start | bytes 3407872
  254.9 206.8 %reduce-scatter.17.cloned.1.call-start = ((), (), s32[]{:S(2)}) async-start(), calls=%async_computation.9 | async-start | bytes 2654208 | tf_op jit(solution)/shard_map/reduce_scatter | solution.py:901
  257.6 276.2 %reduce-scatter.11.cloned.1.call-start = ((), (), s32[]{:S(2)}) async-start(), calls=%async_computation.6 | async-start | bytes 2654208 | tf_op jit(solution)/shard_map/reduce_scatter | solution.py:891
  262.8 437.3 %reduce-scatter.15.cloned.1.call-start = ((), (), s32[]{:S(2)}) async-start(), calls=%async_computation.8 | async-start | bytes 10616832 | tf_op jit(solution)/shard_map/reduce_scatter | solution.py:897
  273.5 593.1 %reduce-scatter.13.cloned.1.call-start = ((), (), s32[]{:S(2)}) async-start(), calls=%async_computation.7 | async-start | bytes 10616832 | tf_op jit(solution)/shard_map/reduce_scatter | solution.py:895
  283.4 673.3 %reduce-scatter.21.cloned.1.call-start = ((), (), s32[]{:S(2)}) async-start(), calls=%async_computation.11 | async-start | bytes 442368
  285.2 581.5 %copy-start.51 = (f32[3]{0:T(128)S(1)}, f32[3]{0:T(128)}, u32[]{:S(2)}) copy-start(f32[3]{0:T(128)} %get-tuple-element.256) | copy-start | bytes 40
  285.2 621.1 %copy-start.54 = (u32[32]{0:T(128)S(1)}, u32[32]{0:T(128)}, u32[]{:S(2)}) copy-start(u32[32]{0:T(128)} %constant.53) | copy-start | bytes 388
  285.2 734.2 %all-reduce.16.cloned.1.call-start = ((), (), s32[]{:S(2)}) async-start(), calls=%async_computation.12 | async-start | bytes 8257536 | tf_op jit(solution)/shard_map/psum | solution.py:905
  866.6 42.2 %copy-start.28 = (f32[768]{0:T(1024)S(1)}, f32[768]{0:T(1024)}, u32[]{:S(2)}) copy-start(f32[768]{0:T(1024)} %get-tuple-element.283) | copy-start | bytes 9220
  866.6 42.2 %copy-start.29 = (f32[768]{0:T(1024)S(1)}, f32[768]{0:T(1024)}, u32[]{:S(2)}) copy-start(f32[768]{0:T(1024)} %get-tuple-element.271) | copy-start | bytes 9220
  866.6 42.2 %copy-start.26 = (f32[768]{0:T(1024)S(1)}, f32[768]{0:T(1024)}, u32[]{:S(2)}) copy-start(f32[768]{0:T(1024)} %get-tuple-element.258) | copy-start | bytes 9220
  866.6 42.2 %copy-start.27 = (f32[768]{0:T(1024)S(1)}, f32[768]{0:T(1024)}, u32[]{:S(2)}) copy-start(f32[768]{0:T(1024)} %get-tuple-element.260) | copy-start | bytes 9220
  866.6 42.2 %copy-start.30 = (f32[768]{0:T(1024)S(1)}, f32[768]{0:T(1024)}, u32[]{:S(2)}) copy-start(f32[768]{0:T(1024)} %get-tuple-element.197) | copy-start | bytes 9220
  866.6 42.2 %copy-start.31 = (f32[3072]{0:T(1024)S(1)}, f32[3072]{0:T(1024)}, u32[]{:S(2)}) copy-start(f32[3072]{0:T(1024)} %get-tuple-element.281) | copy-start | bytes 36868
  866.6 42.2 %copy-start.34 = (f32[768]{0:T(1024)S(1)}, f32[768]{0:T(1024)}, u32[]{:S(2)}) copy-start(f32[768]{0:T(1024)} %get-tuple-element.285) | copy-start | bytes 9220
  866.6 42.2 %copy-start.35 = (f32[768]{0:T(1024)S(1)}, f32[768]{0:T(1024)}, u32[]{:S(2)}) copy-start(f32[768]{0:T(1024)} %get-tuple-element.199) | copy-start | bytes 9220
  866.7 42.2 %copy-start.36 = (f32[768]{0:T(1024)S(1)}, f32[768]{0:T(1024)}, u32[]{:S(2)}) copy-start(f32[768]{0:T(1024)} %get-tuple-element.202) | copy-start | bytes 9220
  956.7 65.4 %copy-start.12 = (bf16[1024,768]{1,0:T(8,128)(2,1)S(1)}, bf16[1024,768]{1,0:T(8,128)(2,1)}, u32[]{:S(2)}) copy-start(bf16[1024,768]{1,0:T(8,128)(2,1)} %get-tuple-element.407) | copy-start | bytes 4718596
  (50 other events, 133.6 us)
Sparse Core Ops, SparseCore 0:
  255.1 134.5 reduce-scatter.18
  393.6 68.0 reduce-scatter.16
  465.6 68.0 reduce-scatter.10
  537.6 162.4 reduce-scatter.14
  704.0 162.5 reduce-scatter.12
  870.6 60.5 reduce-scatter.20
  934.8 84.5 all-reduce.15

commit v2 on v1

--- a/solution.py
+++ b/solution.py
@@ -316,7 +316,7 @@
     if comm:
         save(w1, w1_h)
 
-    tile = 256
+    tile = rows // nz
     zero_row = jnp.zeros((1, width), F32)
     biases = (vec_o[0:1, :], zero_row, vec_o[1:2, :])
 
@@ -367,7 +367,7 @@
             w = w2[:, :, :, (b + 1) * width : (b + 2) * width].reshape(width, width)
             a, g = gelu_both(nn(low, w) + ib_o[0:1, b * width : (b + 1) * width])
             act[r, cols] = a.astype(BF16)
-            dg[r, cols] = g.astype(BF16)
+            dg[i, :, :, b * width : (b + 1) * width] = g.astype(BF16).reshape(2, tile // 2, width)
         for n in range(rows // tile):
             for step in steps3[4 + 2 * n : 6 + 2 * n]:
                 pl.when(i == n)(step)
@@ -439,7 +439,7 @@
         (S((rows, width), BF16), any_),
         (S((rows, width), BF16), any_),
         (S((rows, ff), BF16), any_),
-        (S((rows, ff), BF16), any_),
+        (S((nz, 2, rows // (2 * nz), ff), BF16), any_),
         (S((rows, width), BF16), any_),
         (S((2, rows, 128), F32), vm),
         (S((8 * (rows // span), width), F32), vm),
@@ -458,7 +458,7 @@
         V((rows, width), BF16),
         V((rows, width), BF16),
         V((rows, ff), BF16),
-        V((rows, ff), BF16),
+        V((nz, 2, rows // (2 * nz), ff), BF16),
         V((rows, width), BF16),
         V((rows, width), BF16),
         D((24,)), D((nf,)), D((nf,)),
@@ -482,6 +482,617 @@
         tokens, lengths, *gathered, smalls)
 
 
+def attend_backward(kv, gctx, lse, lengths, s, hp, span, width, size):
+    wide = 2 * size
+    pairs = width // wide
+    rows = pl.ds(pl.multiple_of(s * span, span), span)
+
+    def cols(p):
+        return pl.ds(pl.multiple_of(p * width + hp * wide, wide), wide)
+
+    q, k, v = (kv[rows, cols(p)] for p in range(3))
+    g = gctx[rows, cols(0)]
+    logs = lse[s * pairs + hp]
+    lane = lax.broadcasted_iota(jnp.int32, (span, wide), 1)
+    slot = lax.broadcasted_iota(jnp.int32, (span, wide), 0)
+    fill = jnp.where(slot < lengths[s], 0.0, NEG).astype(BF16)
+    scale = size ** (-0.5)
+    factor = scale * LOG2E
+    kt = k.T
+    gqs, gks, gvs = [], [], []
+    for h in range(2):
+        mine = lane < size if h == 0 else lane >= size
+        other = (1 - h) * size
+        qh = jnp.where(mine, q, jnp.where(lane == other, 1.0, 0.0).astype(BF16))
+        kh = jnp.where(mine, k, fill)
+        vh = jnp.where(mine, v, jnp.zeros_like(v))
+        p = jnp.exp2(nt(kh, qh) * factor - logs[h : h + 1, :])
+        gvs.append(nn(p.astype(BF16), g))
+        gp = nt(vh, g)
+        delta = jnp.sum(gp * p, axis=0, keepdims=True)
+        gs = (p * (gp - delta)).astype(BF16)
+        gks.append(nn(gs, q))
+        gqs.append(nn(kt, gs)[h * size : (h + 1) * size, :])
+    kv[rows, cols(0)] = (jnp.concatenate(gqs, axis=0).T * scale).astype(BF16)
+    kv[rows, cols(1)] = (jnp.where(lane < size, gks[0], gks[1]) * scale).astype(BF16)
+    kv[rows, cols(2)] = jnp.where(lane < size, gvs[0], gvs[1]).astype(BF16)
+
+
+class Spread:
+    def __init__(self, buf, send, recv):
+        self.buf, self.send, self.recv = buf, send, recv
+        self.nz = buf.shape[3]
+        self.me = here()
+
+    def copy(self, n, incoming):
+        x, c, z, y = self.me
+        nz = self.nz
+        if n < nz - 1:
+            k = n + 1
+            peer = (x, c, lax.rem(z + k, nz), y)
+            ref = self.buf.at[x, c, y, lax.rem(z + nz - k, nz) if incoming else z]
+        elif n == nz - 1:
+            peer = (x, c, z, 1 - y)
+            ref = self.buf.at[x, c, 1 - y if incoming else y]
+        elif n == nz:
+            peer = (1 - x, c, z, y)
+            ref = self.buf.at[1 - x if incoming else x, c]
+        else:
+            peer = (x, 1 - c, z, y)
+            ref = self.buf.at[:, 1 - c if incoming else c]
+        return pltpu.make_async_remote_copy(
+            src_ref=ref, dst_ref=ref, send_sem=self.send.at[n], recv_sem=self.recv.at[n], device_id=at(*peer), device_id_type=MESH
+        )
+
+    def step(self, j):
+        nz = self.nz
+        if j == 0:
+            for n in range(nz - 1):
+                self.copy(n, False).start()
+            return
+        if j == 1:
+            for n in range(nz - 1):
+                self.copy(n, True).wait_recv()
+        else:
+            self.copy(nz + j - 3, True).wait_recv()
+        if j < 4:
+            self.copy(nz + j - 2, False).start()
+
+    def drain(self):
+        for n in range(self.nz + 2):
+            self.copy(n, False).wait_send()
+
+
+class Scatter:
+    def __init__(self, refs, out, send, recv):
+        self.g, self.r1, self.ry1, self.rx1, self.rx2, self.ry2, self.rz = refs
+        self.out, self.send, self.recv = out, send, recv
+        self.nz, _, self.r, self.cols = self.g.shape
+        self.x, self.c, self.z, self.y = here()
+        half = self.cols // 2
+        a1 = self.ry1.shape[-1]
+        r2 = self.r // 2
+        self.rows = pl.ds(pl.multiple_of(self.x * r2, 16), r2)
+        self.rows_o = pl.ds(pl.multiple_of((1 - self.x) * r2, 16), r2)
+        self.mine = pl.ds(pl.multiple_of(self.c * half, 128), half)
+        self.theirs = pl.ds(pl.multiple_of((1 - self.c) * half, 128), half)
+        self.a1 = pl.ds(pl.multiple_of(self.c * half, 128), a1)
+        self.a2 = pl.ds(pl.multiple_of(self.c * half + a1, 128), half - a1)
+
+    def copy(self, n):
+        x, c, z, y = self.x, self.c, self.z, self.y
+        g, out = self.g, self.out
+        core, xn, yn = (x, 1 - c, z, y), (1 - x, c, z, y), (x, c, z, 1 - y)
+        if n == 0:
+            src, dst, peer = g.at[:, :, :, self.theirs], self.r1, core
+        elif n == 1:
+            src, dst, peer = g.at[:, 1 - y, :, self.a1], self.ry1, yn
+        elif n == 2:
+            src, dst, peer = g.at[:, :, self.rows_o, self.a2], self.rx2, xn
+        elif n == 3:
+            src, dst, peer = g.at[:, y, self.rows_o, self.a1], self.rx1, xn
+        elif n == 4:
+            src, dst, peer = g.at[:, 1 - y, self.rows, self.a2], self.ry2, yn
+        elif n < 4 + self.nz:
+            k = n - 4
+            zk = lax.rem(z + k, self.nz)
+            src, dst, peer = g.at[zk, y, self.rows, self.mine], self.rz.at[k - 1], (x, c, zk, y)
+        elif n == 4 + self.nz:
+            src = dst = out.at[self.rows, self.mine]
+            peer = xn
+        else:
+            src = dst = out.at[:, self.mine]
+            peer = core
+        return pltpu.make_async_remote_copy(
+            src_ref=src, dst_ref=dst, send_sem=self.send.at[n], recv_sem=self.recv.at[n], device_id=at(*peer), device_id_type=MESH
+        )
+
+    def got(self, n):
+        if n < 4 + self.nz:
+            self.copy(n).wait_recv()
+            return
+        if n == 4 + self.nz:
+            ref, peer = self.out.at[self.rows_o, self.mine], (1 - self.x, self.c, self.z, self.y)
+        else:
+            ref, peer = self.out.at[:, self.theirs], (self.x, 1 - self.c, self.z, self.y)
+        pltpu.make_async_remote_copy(
+            src_ref=ref, dst_ref=ref, send_sem=self.send.at[n], recv_sem=self.recv.at[n], device_id=at(*peer), device_id_type=MESH
+        ).wait_recv()
+
+    def step(self, j):
+        g, y, nz = self.g, self.y, self.nz
+        last = 4 + nz
+        if j == 0:
+            self.copy(0).start()
+        elif j == 1:
+            self.got(0)
+
+            def add(i, _):
+                for yy in range(2):
+                    g[i, yy, :, self.mine] = g[i, yy, :, self.mine] + self.r1[i, yy]
+                return 0
+
+            lax.fori_loop(0, nz, add, 0)
+            self.copy(1).start()
+            self.copy(2).start()
+        elif j == 2:
+            self.got(1)
+
+            def add(i, _):
+                g[i, y, :, self.a1] = g[i, y, :, self.a1] + self.ry1[i]
+                return 0
+
+            lax.fori_loop(0, nz, add, 0)
+            self.copy(3).start()
+            self.got(2)
+
+            def add(i, _):
+                for yy in range(2):
+                    g[i, yy, self.rows, self.a2] = g[i, yy, self.rows, self.a2] + self.rx2[i, yy]
+                return 0
+
+            lax.fori_loop(0, nz, add, 0)
+            self.copy(4).start()
+        elif j == 3:
+            self.got(3)
+            self.got(4)
+
+            def add(i, _):
+                g[i, y, self.rows, self.a1] = g[i, y, self.rows, self.a1] + self.rx1[i]
+                g[i, y, self.rows, self.a2] = g[i, y, self.rows, self.a2] + self.ry2[i]
+                return 0
+
+            lax.fori_loop(0, nz, add, 0)
+            for k in range(1, nz):
+                self.copy(4 + k).start()
+        elif j == 4:
+            total = g[self.z, y, self.rows, self.mine].astype(F32)
+            for k in range(1, nz):
+                self.got(4 + k)
+                total += self.rz[k - 1].astype(F32)
+            self.out[self.rows, self.mine] = total.astype(BF16)
+            self.copy(last).start()
+        elif j == 5:
+            self.got(last)
+            self.copy(last + 1).start()
+        else:
+            self.got(last + 1)
+
+    def drain(self):
+        for n in range(6 + self.nz):
+            self.copy(n).wait_send()
+
+
+def backward_kernel(comm, lengths, labels, cb, vec, lse, first, inv_h, cot_h, tok_h, w1_h, w2_h, w3_h, qkv_h, ctx_h, hid_h, u1_h, act_h, dg_h, u2_h,
+                    loss_o, own_o, ib_o, pool_o, class_o, wo_o, wi_o, wu_o, wq_o, tg_h,
+                    A, D, w2, w3, cot, u2, u1, hid, gffn, gr, inv, acc, gfirst,
+                    G, R1, Ry1, Rx1, Rx2, Ry2, Rz, early, late, loc, free, s_rs, r_rs, s_sp, r_sp):
+    x, c, z, y = here() if comm else (0, 0, 0, 0)
+    rows, width = cot.shape
+    seqs = lengths.shape[0]
+    span = rows // seqs
+    ff = A.shape[1]
+    size = width // HEADS
+    nz = D.shape[0]
+    tile = rows // nz
+    nb = ff // width
+    part = width // (2 * nz)
+    fr = ff // (2 * nz)
+    loads = {}
+
+    def load(name, src, dst):
+        cp = pltpu.make_async_copy(src, dst, loc.at[len(loads)])
+        cp.start()
+        loads[name] = cp
+
+    load("cot", cot_h, cot)
+    load("u2", u2_h, u2)
+    load("inv2", inv_h.at[1], inv)
+    load("w3", w3_h, w3)
+    load("act", act_h, A)
+    load("dg", dg_h, D)
+    load("hid", hid_h, hid)
+    load("w2", w2_h, w2)
+    load("u1", u1_h, u1)
+
+    if comm:
+        barrier = pltpu.get_barrier_semaphore()
+        peers = [(x, c, lax.rem(z + k, nz), y) for k in range(1, nz)]
+        peers += [(x, c, z, 1 - y), (1 - x, c, z, y), (x, 1 - c, z, y)]
+        for p in peers:
+            pl.semaphore_signal(barrier, inc=1, device_id=at(*p), device_id_type=MESH)
+        pl.semaphore_wait(barrier, len(peers))
+
+        def outer_out(b):
+            return wu_o.at[pl.ds(pl.multiple_of(b * part, 16), part), :]
+
+        def inner_out(b):
+            return wi_o.at[:, pl.ds(pl.multiple_of(b * width, 128), width)]
+
+        def block(n, out):
+            return Scatter([G.at[n], R1.at[n], Ry1.at[n], Rx1.at[n], Rx2.at[n], Ry2.at[n], Rz.at[n]], out, s_rs.at[n], r_rs.at[n])
+
+        def late_block(q):
+            n = 2 * nb + q
+            h, t, e, hr = width // 2, width // 3, width // 6, part // 2
+            refs = [
+                D.at[:, :, pl.ds(0, part), pl.ds(q * width, width)],
+                w2.at[:, :, :, pl.ds(q * h, h)],
+                w2.at[:, 0, :, pl.ds(2 * width + q * t, t)],
+                w2.at[:, 1, pl.ds(0, hr), pl.ds(2 * width + q * t, t)],
+                w2.at[:, :, pl.ds(0, hr), pl.ds(2 * width + 4 * t + q * e, e)],
+                w2.at[:, 1, pl.ds(hr, hr), pl.ds(2 * width + q * e, e)],
+                w2.at[pl.ds(0, nz - 1), q // 2, pl.ds(hr, hr), pl.ds(2 * width + 4 * t + (q % 2) * h, h)],
+            ]
+            return Scatter(refs, wo_o if q == 0 else wq_o.at[q - 1], s_rs.at[n], r_rs.at[n])
+
+        def each(first_block, count, make, j):
+            def body(b, _):
+                block(first_block + b, make(b)).step(j)
+                return 0
+
+            lax.fori_loop(0, count, body, 0)
+
+        early_ag = Spread(early, s_sp.at[0], r_sp.at[0])
+        late_ag = Spread(late, s_sp.at[1], r_sp.at[1])
+
+        def step(name, j):
+            if name == "outer":
+                each(0, nb, outer_out, j)
+            elif name == "inner0":
+                each(nb, nb // 2, inner_out, j)
+            elif name == "inner1":
+                each(nb + nb // 2, nb // 2, lambda b: inner_out(b + nb // 2), j)
+            elif name == "out":
+                late_block(0).step(j)
+            elif name == "early":
+                early_ag.step(j)
+            elif name == "late":
+                late_ag.step(j)
+            else:
+                late_block(name + 1).step(j)
+    else:
+        def step(name, j):
+            pass
+
+    def steps(*pairs):
+        for name, j in pairs:
+            step(name, j)
+
+    def hooks(i, table):
+        for n, pairs in enumerate(table):
+            if pairs and comm:
+                pl.when(i == n)(functools.partial(steps, *pairs))
+
+    acc[...] = jnp.zeros_like(acc)
+
+    loads["w3"].wait()
+    lane = lax.broadcasted_iota(jnp.int32, (8 * seqs, 128), 1)
+    row = lax.broadcasted_iota(jnp.int32, (8 * seqs, 128), 0)
+    live = (lane >= 1) & (lane < 4)
+    w_pool = w3[:, :, fr:, :].reshape(width, width)
+    first_low = first[...].astype(BF16)
+    pooled = jnp.tanh(nn(first_low, w_pool) + vec[8:9, :])
+    pooled_low = pooled.astype(BF16)
+    heads = jnp.concatenate([vec[8:16, :], jnp.zeros((120, width), F32)], axis=0).astype(BF16)
+    logits = nt(pooled_low, heads) + cb[0:1, :]
+    peak = jnp.max(jnp.where(live, logits, -3.0e38), axis=-1, keepdims=True)
+    mass = jnp.where(live, jnp.exp(logits - peak), 0.0)
+    logsum = peak + jnp.log(jnp.sum(mass, axis=-1, keepdims=True))
+    label = jnp.full((8 * seqs, 128), labels[0])
+    for s in range(1, seqs):
+        label = jnp.where(row >= 8 * s, labels[s], label)
+    onehot = jnp.where(lane == label + 1, 1.0, 0.0)
+    loss_o[...] = jnp.broadcast_to(logsum - jnp.sum(onehot * logits, axis=-1, keepdims=True), loss_o.shape)
+    g_logits = jnp.where(live & (row % 8 == 0), jnp.exp(logits - logsum) - onehot, 0.0).astype(BF16)
+    g_pre = (nn(g_logits, heads) * (1.0 - pooled * pooled)).astype(BF16)
+    gfirst[...] = nt(g_pre, w_pool)
+
+    loads["cot"].wait()
+    loads["u2"].wait()
+    loads["inv2"].wait()
+    gain2, gain1 = vec[6:7, :], vec[3:4, :]
+
+    def colsum(v):
+        return jnp.sum(v, axis=0, keepdims=True)
+
+    per = span // tile
+
+    def second_norm(i, _):
+        r = pl.ds(pl.multiple_of(i * tile, tile), tile)
+        s, j = i // per, i % per
+        slot = lax.broadcasted_iota(jnp.int32, (tile, width), 0) + j * tile
+        gl = jnp.where(slot < lengths[s], cot[r, :].astype(F32), 0.0)
+        head = gfirst[pl.ds(pl.multiple_of(8 * s, 8), 8), :] * jnp.where(j == 0, 1.0, 0.0)
+        gl = gl + jnp.concatenate([head, jnp.zeros((tile - 8, width), F32)], axis=0)
+        u = u2[r, :].astype(F32)
+        a = gl * gain2
+        iv = inv[r, :]
+        g2 = (a - rowmean(a) - u * rowmean(a * u)) * iv[:, :1]
+        gr[r, :] = g2
+        low = g2.astype(BF16)
+        gffn[r, :] = low
+        acc[3:4, :] += colsum(low.astype(F32))
+        acc[4:5, :] += colsum(gl * u)
+        acc[5:6, :] += colsum(gl)
+        return 0
+
+    lax.fori_loop(0, rows // tile, second_norm, 0)
+    load("tok", tok_h, u2)
+    load("inv1", inv_h.at[0], inv)
+
+    loads["act"].wait()
+
+    def outer_grad(f, _):
+        part_of = tn(A[:, pl.ds(pl.multiple_of(f * fr, 128), fr)], gffn[...]).astype(BF16)
+        for b in range(nb):
+            G[b, f // 2, f % 2] = part_of[b * part : (b + 1) * part, :]
+        return 0
+
+    lax.fori_loop(0, 2 * nz, outer_grad, 0)
+    load("qkv", qkv_h, A.at[:, pl.ds(0, 3 * width)])
+    load("ctx", ctx_h, A.at[:, pl.ds(3 * width, width)])
+    steps(("outer", 0))
+
+    loads["dg"].wait()
+
+    def inner_back(i, _):
+        r = pl.ds(pl.multiple_of(i * tile, tile), tile)
+        for b in range(nb):
+            cols = slice(b * width, (b + 1) * width)
+            w = w3[b, :, :fr, :].reshape(width, width)
+            g = nt(gffn[r, :], w) * D[i, :, :, cols].reshape(tile, width).astype(F32)
+            low = g.astype(BF16)
+            D[i, :, :, cols] = low.reshape(2, tile // 2, width)
+            acc[6 + b : 7 + b, :] += colsum(low.astype(F32))
+        hooks(i, [[], [], [("outer", 1)]])
+        return 0
+
+    lax.fori_loop(0, rows // tile, inner_back, 0)
+    for p in range(3):
+        load(("w1", p), w1_h.at[:, :, :, pl.ds(p * width, width)], w3.at[:, :, pl.ds(p * part, part), :])
+
+    loads["hid"].wait()
+
+    def inner_grad(b, _):
+        cols = pl.ds(pl.multiple_of(b * width, width), width)
+        for m in range(2):
+            h = width // 2
+            got = tn(hid[:, m * h : (m + 1) * h], D[:, :, :, cols].reshape(rows, width)).astype(BF16)
+            G[nb + b, m * nz // 2 : (m + 1) * nz // 2] = got.reshape(nz // 2, 2, part, width)
+        hooks(b, [[], [("inner0", 0), ("outer", 2)], [], [("inner1", 0), ("inner0", 1)]])
+        return 0
+
+    lax.fori_loop(0, nb, inner_grad, 0)
+
+    loads["w2"].wait()
+    loads["u1"].wait()
+    loads["inv1"].wait()
+
+    def first_norm(i, _):
+        r = pl.ds(pl.multiple_of(i * tile, tile), tile)
+        gh = gr[r, :]
+        for b in range(nb):
+            w = w2[:, :, :, (b + 1) * width : (b + 2) * width].reshape(width, width)
+            gh += nt(D[i, :, :, b * width : (b + 1) * width].reshape(tile, width), w)
+        u = u1[r, :].astype(F32)
+        a = gh * gain1
+        iv = inv[r, :]
+        g1 = (a - rowmean(a) - u * rowmean(a * u)) * iv[:, :1]
+        gr[r, :] = g1
+        low = g1.astype(BF16)
+        cot[r, :] = low
+        acc[0:1, :] += colsum(low.astype(F32))
+        acc[1:2, :] += colsum(gh * u)
+        acc[2:3, :] += colsum(gh)
+        w = w2[:, :, :, :width].reshape(width, width)
+        gffn[r, :] = nt(low, w).astype(BF16)
+        hooks(i, [[("outer", 3)], [("inner1", 1)], [("inner0", 2)], [("outer", 4)]])
+        return 0
+
+    lax.fori_loop(0, rows // tile, first_norm, 0)
+    if comm:
+        for p in peers:
+            pl.semaphore_signal(free, inc=1, device_id=at(*p), device_id_type=MESH)
+        pay = jnp.concatenate(
+            [acc[0:10, :]]
+            + [first_low[8 * s : 8 * s + 1, :].astype(F32) for s in range(seqs)]
+            + [g_pre[8 * s : 8 * s + 1, :].astype(F32) for s in range(seqs)]
+            + [pooled_low[8 * s : 8 * s + 1, :].astype(F32) for s in range(seqs)],
+            axis=0,
+        )
+        early[x, c, y, z] = pay.astype(BF16)
+
+    loads["ctx"].wait()
+    loads["qkv"].wait()
+    for m in range(2):
+        h = width // 2
+        got = tn(A[:, 3 * width + m * h : 3 * width + (m + 1) * h], cot[...]).astype(BF16)
+        D[m * nz // 2 : (m + 1) * nz // 2, :, :part, :width] = got.reshape(nz // 2, 2, part, width)
+    if comm:
+        pl.semaphore_wait(free, len(peers))
+    steps(("out", 0), ("early", 0), ("inner1", 2), ("inner0", 3))
+
+    loads["tok"].wait()
+    groups = 3
+    pairs = HEADS // 2
+    gp = pairs // groups
+    wide = gp * 2 * size
+    tables = [
+        [[("out", 1)], [("inner0", 4), ("early", 1)], [("inner1", 3), ("out", 2)], [("inner1", 4), ("early", 2)]],
+        [[(0, 1), ("early", 3)], [("out", 3)], [(0, 2)], [("out", 4), ("early", 4)]],
+        [[(1, 1), (0, 3)], [("outer", 5), ("inner0", 5)], [(1, 2), (0, 4)], [("inner1", 5), ("out", 5)]],
+    ]
+    for q in range(groups):
+        def attention(i, _):
+            attend_backward(A, gffn, lse, lengths, i // gp, q * gp + i % gp, span, width, size)
+            hooks(i, tables[q])
+            return 0
+
+        lax.fori_loop(0, seqs * gp, attention, 0)
+        for p in range(3):
+            block_of = A[:, p * width + q * wide : p * width + (q + 1) * wide]
+            got = tn(u2[...], block_of).astype(BF16)
+            D[:, :, :part, (q + 1) * width + p * wide : (q + 1) * width + (p + 1) * wide] = got.reshape(nz, 2, part, wide)
+            if p != 1:
+                acc[10 + p // 2 : 11 + p // 2, q * wide : (q + 1) * wide] = colsum(block_of.astype(F32))
+        steps((q, 0))
+    if comm:
+        tilerows = [acc[10 + n : 11 + n, j * 128 : (j + 1) * 128] for n in range(2) for j in range(width // 128)]
+        tilerows += [g_logits[8 * s : 8 * s + 1, :].astype(F32) for s in range(seqs)]
+        tilerows.append(jnp.zeros((16 - len(tilerows), 128), F32))
+        late[x, c, y, z] = jnp.concatenate(tilerows, axis=0).astype(BF16)
+    steps(("late", 0))
+
+    for p in range(3):
+        loads[("w1", p)].wait()
+
+    def input_grad(i, _):
+        r = pl.ds(pl.multiple_of(i * tile, tile), tile)
+        g = gr[r, :]
+        for p in range(3):
+            w = w3[:, :, p * part : (p + 1) * part, :].reshape(width, width)
+            g += nt(A[r, p * width : (p + 1) * width], w)
+        cot[r, :] = g.astype(BF16)
+        hooks(i, [[(2, 1), (1, 3), ("late", 1)], [(2, 2), ("late", 2), (1, 4)], [(0, 5), ("late", 3), (2, 3)], [(2, 4), (1, 5), ("late", 4)]])
+        return 0
+
+    lax.fori_loop(0, rows // tile, input_grad, 0)
+    back = pltpu.make_async_copy(cot, tg_h, loc.at[len(loads)])
+    back.start()
+    if comm:
+        n = 4 * 2 * nz
+        def slot_of(i):
+            return (i // (4 * nz), i // (2 * nz) % 2, i // nz % 2, i % nz)
+
+        total = lax.fori_loop(0, n, lambda i, t: t + early[slot_of(i)].astype(F32), jnp.zeros((16, width), F32))
+        lates = late[...].reshape(n, 16, 128)
+        lsum = jnp.sum(lates.astype(F32), axis=0)
+        six = width // 128
+        qb = jnp.concatenate([lsum[j : j + 1, :] for j in range(six)], axis=1)
+        vb = jnp.concatenate([lsum[six + j : six + j + 1, :] for j in range(six)], axis=1)
+        r16 = lax.broadcasted_iota(jnp.int32, (16, width), 0)
+        total = jnp.where(r16 == 10, qb, jnp.where(r16 == 11, vb, total))
+        f = z * 2 + y
+        src = lax.broadcasted_iota(jnp.int32, (width, 128), 0)
+        dst = lax.broadcasted_iota(jnp.int32, (width, 128), 1)
+        pick = jnp.where((src == dst + f * part) & (dst < part), 1.0, 0.0).astype(BF16)
+        src = lax.broadcasted_iota(jnp.int32, (width, fr), 0)
+        dst = lax.broadcasted_iota(jnp.int32, (width, fr), 1)
+        pick_ff = jnp.where(src == dst + y * fr, 1.0, 0.0).astype(BF16)
+        high = total.astype(BF16)
+        rest = (total - high.astype(F32)).astype(BF16)
+        own = nn(high, pick) + nn(rest, pick)
+        wide_own = nn(high, pick_ff) + nn(rest, pick_ff)
+        r16f = lax.broadcasted_iota(jnp.int32, (16, fr), 0)
+        ib_o[...] = jnp.broadcast_to(colsum(jnp.where(r16f == 6 + z, wide_own, 0.0)), ib_o.shape)
+        flat = early[...].reshape(n * 16, width)
+        chosen = nn(flat, pick)
+        rid = lax.broadcasted_iota(jnp.int32, (n * 16, 128), 0) % 16
+        firsts = pltpu.roll(jnp.where((rid >= 10) & (rid < 10 + seqs), chosen, 0.0), seqs, 0).astype(BF16)
+        pool_o[...] = tn(firsts, flat)
+        pooleds = pltpu.roll(jnp.where(rid >= 10 + 2 * seqs, chosen, 0.0), n * 16 - seqs, 0).astype(BF16)
+        class_o[...] = tn(pooleds, lates.reshape(n * 16, 128))
+        middle = (rid >= 10 + seqs) & (rid < 10 + 2 * seqs)
+        pb = colsum(jnp.where(middle, chosen, 0.0))
+        cbg = colsum(jnp.where(middle, lates.reshape(n * 16, 128).astype(F32), 0.0))
+        r16s = lax.broadcasted_iota(jnp.int32, (16, 128), 0)
+        own_o[...] = jnp.where(r16s == 12, pb, jnp.where(r16s == 13, cbg, own))
+        steps((2, 5), ("outer", 6), ("inner0", 6), ("inner1", 6), ("out", 6), (0, 6), (1, 6), (2, 6))
+        early_ag.drain()
+        late_ag.drain()
+
+        def finish(b, _):
+            block(b, wo_o).drain()
+            return 0
+
+        lax.fori_loop(0, 2 * nb, finish, 0)
+        for q in range(groups + 1):
+            late_block(q).drain()
+    back.wait()
+
+
+def backward(lengths, labels, cb, vec, lse, inv, first, cot, tok, w1, w2, w3, qkv, ctx, hid, u1, act, dg, u2, comm=True):
+    rows, width = cot.shape
+    nz = w1.shape[0]
+    ff = act.shape[1]
+    part = width // (2 * nz)
+    fr = ff // (2 * nz)
+    nb = ff // width
+    seqs = lengths.shape[0]
+    any_, vm, smem = (pl.BlockSpec(memory_space=m) for m in (pl.ANY, pltpu.VMEM, pltpu.SMEM))
+    S = jax.ShapeDtypeStruct
+    outs = [
+        (S((8 * seqs, 128), F32), vm),
+        (S((16, 128), F32), vm),
+        (S((8, fr), F32), vm),
+        (S((128, width), F32), vm),
+        (S((128, 128), F32), vm),
+        (S((part, width), BF16), vm),
+        (S((part, ff), BF16), vm),
+        (S((fr, width), BF16), vm),
+        (S((3, part, width), BF16), vm),
+        (S((rows, width), BF16), any_),
+    ]
+    V = pltpu.VMEM
+    D = pltpu.SemaphoreType.DMA
+    n = 2 * nb
+    half, third = width // 2, width // 3
+    scratch = [
+        V((rows, ff), BF16),
+        V(dg.shape, BF16),
+        V((nz, 2, part, width + ff), BF16),
+        V((nz, 2, fr + part, width), BF16),
+        V((rows, width), BF16),
+        V((rows, width), BF16),
+        V((rows, width), BF16),
+        V((rows, width), BF16),
+        V((rows, width), BF16),
+        V((rows, width), F32),
+        V((rows, 128), F32),
+        V((16, width), F32),
+        V((8 * seqs, width), F32),
+        V((n, nz, 2, part, width), BF16),
+        V((n, nz, 2, part, half), BF16),
+        V((n, nz, part, third), BF16),
+        V((n, nz, part // 2, third), BF16),
+        V((n, nz, 2, part // 2, third // 2), BF16),
+        V((n, nz, part // 2, third // 2), BF16),
+        V((n, nz - 1, part // 2, half), BF16),
+        V((2, 2, 2, nz, 16, width), BF16),
+        V((2, 2, 2, nz, 16, 128), BF16),
+        D((24,)),
+        pltpu.SemaphoreType.REGULAR,
+        D((n + 4, nz + 6)), D((n + 4, nz + 6)), D((2, nz + 2)), D((2, nz + 2)),
+    ]
+    params = pltpu.CompilerParams(vmem_limit_bytes=63 * 2**20, has_side_effects=True, **({"collective_id": 1} if comm else {}))
+    cost = pl.CostEstimate(flops=4 * rows * width * (4 * width + 2 * ff), bytes_accessed=10**7, transcendentals=0)
+    return pl.pallas_call(
+        functools.partial(backward_kernel, comm), out_shape=[o[0] for o in outs], out_specs=[o[1] for o in outs],
+        in_specs=[smem, smem] + [vm] * 4 + [any_] * 13, scratch_shapes=scratch, compiler_params=params, cost_estimate=cost,
+    )(lengths, labels, cb, vec, lse, first, inv, cot, tok, w1, w2, w3, qkv, ctx, hid, u1, act, dg, u2)
+
+
 def normalize(value, gain, shift):
     mean = jnp.mean(value, axis=-1, keepdims=True)
     centred = value - mean
@@ -501,7 +1112,7 @@
 
 
 def matmul(left, right):
-    return nn(left, right)
+    return jnp.dot(left, right, preferred_element_type=jnp.float32)
 
 
 def transposed_left(left, right):
@@ -802,149 +1413,24 @@
     first_gain, first_shift, inner_weight, inner_bias, outer_weight, outer_bias, second_gain, second_shift,
     pool_weight, pool_bias, class_weight, class_bias):
     part = query_bias.shape[0]
+    classes = class_bias.shape[0]
     vectors = jnp.stack([query_bias, value_bias, out_bias, first_gain, first_shift, outer_bias, second_gain, second_shift, pool_bias]
-                        + [class_weight[:, j] for j in range(class_weight.shape[1])])
+                        + [class_weight[:, j] for j in range(classes)])
     smalls = jnp.concatenate([jnp.pad(vectors, ((0, 0), (0, 128 - part))), inner_bias.reshape(-1, 128), jnp.zeros((1, 128), BF16)])
     (output, w1, w2, w3, vec, ib, qkv, context, lse, hidden_low, unit_first, act, dgelu, unit_second, inv, firsts) = forward(
         tokens, lengths, qkv_weight, out_weight, inner_weight, outer_weight, pool_weight, smalls, nz)
-    seqs = lengths.shape[0]
-    rows, width = tokens.shape
-    ff = act.shape[1]
-    span = rows // seqs
-    size = width // HEADS
-    classes = class_bias.shape[0]
-    w_qkv = w1.reshape(width, 3 * width)
-    w2 = w2.reshape(width, width + ff)
-    w_out, w_inner = w2[:, :width], w2[:, width:]
-    fr = ff // (2 * nz)
-    w_outer = w3[:, :, :fr].reshape(ff, width)
-    w_pool = w3[:, :, fr:].reshape(width, width)
-    g_first, g_second, b_pool, w_class = vec[3], vec[6], vec[8], vec[9:12].T.astype(BF16)
-    b_class = class_bias.astype(jnp.float32)
-    unit_first, unit_second = unit_first.astype(F32), unit_second.astype(F32)
-    inverse_first, inverse_second = inv[0, :, :1], inv[1, :, :1]
-    position = lax.broadcasted_iota(jnp.int32, (seqs, span), 1)
-    keep = position < lengths[:, None]
-    valid = keep.reshape(rows, 1).astype(jnp.float32)
-    query = qkv[:, :width].reshape(seqs, span, HEADS, size)
-    key = qkv[:, width : 2 * width].reshape(seqs, span, HEADS, size)
-    value = qkv[:, 2 * width :].reshape(seqs, span, HEADS, size)
-    logsum = (lse[:, :2] / LOG2E).reshape(seqs, HEADS, span)
-    first = firsts[::8].astype(BF16)
-    pooled = jnp.tanh(matmul(first, w_pool) + b_pool)
-    pooled_low = pooled.astype(jnp.bfloat16)
-    logits = matmul(pooled_low, w_class) + b_class
-    peak = jnp.max(logits, axis=-1, keepdims=True)
-    logsum_class = peak + jnp.log(jnp.sum(jnp.exp(logits - peak), axis=-1, keepdims=True))
-    onehot = (labels[:, None] == lax.broadcasted_iota(jnp.int32, (seqs, classes), 1)).astype(
-        jnp.float32
-    )
-    exit_loss = logsum_class[:, 0] - jnp.sum(onehot * logits, axis=-1)
-    grad_logits = (jnp.exp(logits - logsum_class) - onehot).astype(jnp.bfloat16)
-    grad_class_weight = transposed_left(pooled_low, grad_logits)
-    grad_class_local = column_sum(grad_logits)
-    grad_pooled = transposed_right(grad_logits, w_class)
-    grad_pre = (grad_pooled * (1.0 - pooled * pooled)).astype(jnp.bfloat16)
-    grad_pool_weight = transposed_left(first, grad_pre)
-    grad_pool_bias = column_sum(grad_pre)
-    grad_first = transposed_right(grad_pre, w_pool)
-    grad_layer = (cotangent.astype(jnp.float32) * valid).reshape(seqs, span, width)
-    grad_layer = jnp.concatenate(
-        [grad_layer[:, :1] + grad_first[:, None, :], grad_layer[:, 1:]], axis=1
-    )
-    grad_layer = grad_layer.reshape(rows, width)
-    grad_resid_second, grad_second_gain, grad_second_shift = norm_back(
-        grad_layer, unit_second, inverse_second, g_second
-    )
-    grad_ffn = grad_resid_second.astype(jnp.bfloat16)
-    grad_outer_weight = transposed_left(act, grad_ffn)
-    grad_outer_bias = column_sum(grad_ffn)
-    grad_act = transposed_right(grad_ffn, w_outer)
-    grad_inner = (grad_act * dgelu.astype(F32)).astype(jnp.bfloat16)
-    grad_inner_weight = transposed_left(hidden_low, grad_inner)
-    grad_inner_bias = column_sum(grad_inner)
-    grad_hidden = grad_resid_second + transposed_right(grad_inner, w_inner)
-    grad_resid_first, grad_first_gain, grad_first_shift = norm_back(
-        grad_hidden, unit_first, inverse_first, g_first
-    )
-    grad_attended = grad_resid_first.astype(jnp.bfloat16)
-    grad_out_weight = transposed_left(context, grad_attended)
-    grad_out_bias = column_sum(grad_attended)
-    grad_context = (
-        transposed_right(grad_attended, w_out).astype(jnp.bfloat16).reshape(seqs, span, HEADS, size)
-    )
-    grad_query, grad_key, grad_value = lax.map(
-        attend_back, (query, key, value, keep, logsum, grad_context)
-    )
-    grad_query = grad_query.reshape(rows, width)
-    grad_key = grad_key.reshape(rows, width)
-    grad_value = grad_value.reshape(rows, width)
-    grad_qkv = jnp.concatenate([grad_query, grad_key, grad_value], axis=1)
-    grad_qkv_weight = transposed_left(tokens, grad_qkv)
-    grad_query_bias = column_sum(grad_query)
-    grad_value_bias = column_sum(grad_value)
-    tokens_grad = (grad_resid_first + transposed_right(grad_qkv, w_qkv)).astype(jnp.bfloat16)
-    owned = (
-        lax.psum_scatter(grad_qkv_weight, "fsdp", scatter_dimension=0, tiled=True),
-        lax.psum_scatter(grad_query_bias, "fsdp", scatter_dimension=0, tiled=True),
-        lax.psum_scatter(grad_value_bias, "fsdp", scatter_dimension=0, tiled=True),
-        lax.psum_scatter(grad_out_weight, "fsdp", scatter_dimension=0, tiled=True),
-        lax.psum_scatter(grad_out_bias, "fsdp", scatter_dimension=0, tiled=True),
-        lax.psum_scatter(grad_first_gain, "fsdp", scatter_dimension=0, tiled=True),
-        lax.psum_scatter(grad_first_shift, "fsdp", scatter_dimension=0, tiled=True),
-        lax.psum_scatter(grad_inner_weight, "fsdp", scatter_dimension=0, tiled=True),
-        lax.psum_scatter(grad_inner_bias, "fsdp", scatter_dimension=0, tiled=True),
-        lax.psum_scatter(grad_outer_weight, "fsdp", scatter_dimension=0, tiled=True),
-        lax.psum_scatter(grad_outer_bias, "fsdp", scatter_dimension=0, tiled=True),
-        lax.psum_scatter(grad_second_gain, "fsdp", scatter_dimension=0, tiled=True),
-        lax.psum_scatter(grad_second_shift, "fsdp", scatter_dimension=0, tiled=True),
-        lax.psum_scatter(grad_pool_weight, "fsdp", scatter_dimension=0, tiled=True),
-        lax.psum_scatter(grad_pool_bias, "fsdp", scatter_dimension=0, tiled=True),
-        lax.psum_scatter(grad_class_weight, "fsdp", scatter_dimension=0, tiled=True),
-    )
-    summed = lax.psum(
-        (
-            owned[0],
-            owned[1],
-            owned[2],
-            owned[3],
-            owned[4],
-            owned[5],
-            owned[6],
-            owned[7],
-            owned[8],
-            owned[9],
-            owned[10],
-            owned[11],
-            owned[12],
-            owned[13],
-            owned[14],
-            owned[15],
-        ),
-        "dp",
-    )
-    class_bias_grad = lax.psum(grad_class_local, ("dp", "fsdp"))
+    cb = jnp.pad(class_bias.astype(F32)[None, :], ((0, 7), (1, 127 - classes)))
+    (loss, own, ibg, poolg, classg, wo, wi, wu, wq, tokens_grad) = backward(
+        lengths, labels, cb, vec, lse, inv, firsts, cotangent, tokens, w1, w2, w3, qkv, context, hidden_low, unit_first, act, dgelu, unit_second)
+    wide = wq.shape[2] // 3
+    qkv_grad = jnp.concatenate([wq[g, :, p * wide : (p + 1) * wide] for p in range(3) for g in range(3)], axis=1)
+
+    def row(n):
+        return own[n, :part]
+
     return (
-        output,
-        exit_loss,
-        tokens_grad,
-        summed[0],
-        summed[1],
-        summed[2],
-        summed[3],
-        summed[4],
-        summed[5],
-        summed[6],
-        summed[7],
-        summed[8],
-        summed[9],
-        summed[10],
-        summed[11],
-        summed[12],
-        summed[13],
-        summed[14],
-        summed[15],
-        class_bias_grad,
+        output, loss[::8, 0], tokens_grad, qkv_grad.astype(F32), row(10), row(11), wo.astype(F32), row(0), row(1), row(2),
+        wi.astype(F32), ibg[0], wu.astype(F32), row(3), row(4), row(5), poolg[:part], row(12), classg[:part, 1 : 1 + classes], own[13, 1 : 1 + classes],
     )
 
 

time: 1040 us -> 255 us (0.25)
  waiting for transfers between devices: 633 us -> 0 us
  Pallas kernels: 94.4 us -> 229 us
  matrix products: 100 us -> 0 us
  blocking collectives: 84.9 us -> 0 us
  local copies, waits for them, and re-layouts: 76.8 us -> 16.7 us
  other arithmetic: 26.9 us -> 8.17 us
  between operations: 16.5 us -> 0.74 us
    reduce_scatter x4 -> x0, waiting for transfers between devices: 474 us -> none  [the longest x1 166 us: per_device(): lax.psum_scatter(grad_inner_weight, 'fsdp', scatter_dimension=0, tiled=True)]
    pallas_call x0 -> x1, Pallas kernels: none -> 134 us  [backward(): pl.pallas_call(functools.partial(backward_kernel, comm), out_shape=[o[0]...]
    unnamed x9 -> x0, waiting for transfers between devices: 105 us -> none
    dot_general x23 -> x0, matrix products: 99.5 us -> none  [the longest x6 33.5 us: transposed_right(): lax.dot_general(left, right, (((1,), (1,)), ((), ())), preferred_element_...]
    psum x1 -> x0, waiting for transfers between devices: 53.9 us -> none  [per_device(): lax.psum((owned[0], owned[1], owned[2], owned[3], owned[4], owned[5], own...]
    psum x2 -> x0, blocking collectives: 47.3 us -> none  [the longest x1 39.5 us: per_device(): class_bias_grad = lax.psum(grad_class_local, ('dp', 'fsdp'))]
    unnamed x1 -> x0, blocking collectives: 37.6 us -> none
    unnamed x129 -> x21, local copies, waits for them, and re-layouts: 27.7 us -> 7.02 us
  transfers between devices with their start and end apart: 7 -> 0, of which waited for: 6 -> 0; matrix products, arithmetic and copies ran while one was open for 4% -> 0% of each run, Pallas kernels for 0% -> 0%
where the time goes in v2:
time: 255 us; the launch traced here: 254 us
  Pallas kernels  229 us (90%)
  local copies, waits for them, and re-layouts  16.7 us (7%)
  other arithmetic  8.17 us (3%)
    pallas_call x1, Pallas kernels, backward(): pl.pallas_call(functools.partial(backward_kernel, comm), out_shape=[o[0]...  134 us
    pallas_call x1, Pallas kernels, forward(): pl.pallas_call(kern, out_shape=[o[0] for o in outs], out_specs=[o[1] for...  94.4 us
    unnamed x21, local copies, waits for them, and re-layouts  7.02 us

profile of v2, /device:TPU:0, one launch (start us, length us, event | category | flops | bytes accessed | tf_op | source)
XLA Modules:
  0.0 254.3 jit_solution(7541590240607726229)
XLA Ops:
  0.7 0.8 slice_bitcast_fusion.10
  1.5 1.5 stack.39
  3.0 1.3 fusion.2.smalls_h
  4.3 1.3 pad_convert_fusion.cb
  5.7 94.4 %shard_map.356 = (bf16[1024,768]{1,0:T(8,128)(2,1)}, bf16[4,2,96,2304]{3,2,1,0:T(8,128)(2,1)}, bf16[4,2,96,3840]{3,2,1,0:T(8,128)(2,1)}, bf16[4,2,480,768]{3,2,1...) custom-call(bf16[1024,768]{1,0:T(8,128)(2,1)} %tok_h.1, ...), custom_call_target="tpu_custom_call" | custom-call | flops 14495514624 | bytes 10000000 | tf_op jit(solution)/shard_map/pallas_call | solution.py:473
  100.0 134.4 %shard_map.357 = (f32[16,128]{1,0:T(8,128)}, f32[16,128]{1,0:T(8,128)}, f32[8,384]{1,0:T(8,128)}, f32[128,768]{1,0:T(8,128)}, f32[128,128]{1,0:T(8,128)}, /*inde...) custom-call(s32[2]{0:T(128)} %lengths.3, ...), custom_call_target="tpu_custom_call" | custom-call | flops 28991029248 | bytes 10000000 | tf_op jit(solution)/shard_map/pallas_call | solution.py:1090
  234.4 0.8 slice.81
  235.8 1.3 slice_bitcast_fusion
  237.1 1.4 slice_bitcast_fusion.1
  238.5 1.3 slice_reduce_fusion
  239.8 0.9 slice.102
  240.7 0.7 copy.42
  241.3 1.7 convert_element_type.18
  243.0 1.7 slice.100
  244.7 0.8 bitcast_dynamic-update-slice_fusion.8
  245.5 0.8 bitcast_dynamic-update-slice_fusion.7
  246.3 0.8 bitcast_dynamic-update-slice_fusion.6
  247.1 0.8 bitcast_dynamic-update-slice_fusion.5
  248.0 1.0 convert_element_type.17
  249.0 1.1 convert_element_type.19
  250.1 1.1 convert_element_type.20
  251.2 1.1 copy.53
  252.4 0.8 copy-done.1
  253.2 1.1 copy.54
  (16 shorter events, 0.7 us)
Async XLA Ops:
  234.4 13.6 %copy-start.4 = (bf16[3,96,768]{2,1,0:T(8,128)(2,1)S(1)}, bf16[3,96,768]{2,1,0:T(8,128)(2,1)}, u32[]{:S(2)}) copy-start(bf16[3,96,768]{2,1,0:T(8,128)(2,1)} %get-tuple-element.62) | copy-start | bytes 1327108
  241.3 7.7 %copy-start.3 = (bf16[96,3072]{1,0:T(8,128)(2,1)S(1)}, bf16[96,3072]{1,0:T(8,128)(2,1)}, u32[]{:S(2)}) copy-start(bf16[96,3072]{1,0:T(8,128)(2,1)} %get-tuple-element.65) | copy-start | bytes 1769476
  248.0 2.1 copy-start.2
  249.0 2.2 copy-start
  251.2 2.0 copy-start.1
